TPU v7x, 32 devices: a whole 2x2x4 slice. The times are simulated.
32 devices in a mesh: seq: 16 (over z, x, core), ctx: 2 (over y).
Axes of the slice: x: 2, y: 2, z: 4, core: 2. Of those that a mesh axis runs over, the one named last changes fastest.
Arguments:
- tokens: bfloat16 [16384, 1024], P(('seq', 'ctx')), may hold values from -6 to 6
- segments: int32 [16, 1024], P('seq'), may hold values from 0 to 2, as said below
- cotangent: bfloat16 [16384, 1024], P(('seq', 'ctx')), may hold values from -6 to 6
- w_query: bfloat16 [1024, 1024], P(('seq', 'ctx')), may hold values from -0.1875 to 0.1875
- b_query: bfloat16 [1024], P(('seq', 'ctx')), may hold values from -1.1953125 to 1.1953125
- w_key: bfloat16 [1024, 1024], P(('seq', 'ctx')), may hold values from -0.1875 to 0.1875
- w_value: bfloat16 [1024, 1024], P(('seq', 'ctx')), may hold values from -0.1875 to 0.1875
- b_value: bfloat16 [1024], P(('seq', 'ctx')), may hold values from -0.29882812 to 0.29882812
- w_output: bfloat16 [1024, 1024], P(('seq', 'ctx')), may hold values from -3 to 3
- b_output: bfloat16 [1024], P(('seq', 'ctx')), may hold values from -0.59765625 to 0.59765625
- gain_attn: bfloat16 [1024], P(('seq', 'ctx')), may hold values from 0.5 to 1.5
- shift_attn: bfloat16 [1024], P(('seq', 'ctx')), may hold values from -0.59765625 to 0.59765625
- w_inner: bfloat16 [1024, 4096], P(('seq', 'ctx')), may hold values from -0.1875 to 0.1875
- b_inner: bfloat16 [4096], P(('seq', 'ctx')), may hold values from -1.1953125 to 1.1953125
- w_outer: bfloat16 [4096, 1024], P(('seq', 'ctx')), may hold values from -0.09375 to 0.09375
- b_outer: bfloat16 [1024], P(('seq', 'ctx')), may hold values from -0.59765625 to 0.59765625
- gain_ffn: bfloat16 [1024], P(('seq', 'ctx')), may hold values from 0.5 to 1.5
- shift_ffn: bfloat16 [1024], P(('seq', 'ctx')), may hold values from -0.59765625 to 0.59765625
Outputs:
- out_tokens: bfloat16 [16384, 1024], P(('seq', 'ctx'))
- grad_tokens: float32 [16384, 1024], P(('seq', 'ctx'))
- grad_wquery: float32 [1024, 1024], P(('seq', 'ctx'))
- grad_bquery: float32 [1024], P(('seq', 'ctx'))
- grad_wkey: float32 [1024, 1024], P(('seq', 'ctx'))
- grad_wvalue: float32 [1024, 1024], P(('seq', 'ctx'))
- grad_bvalue: float32 [1024], P(('seq', 'ctx'))
- grad_woutput: float32 [1024, 1024], P(('seq', 'ctx'))
- grad_boutput: float32 [1024], P(('seq', 'ctx'))
- grad_gattn: float32 [1024], P(('seq', 'ctx'))
- grad_sattn: float32 [1024], P(('seq', 'ctx'))
- grad_winner: float32 [1024, 4096], P(('seq', 'ctx'))
- grad_binner: float32 [4096], P(('seq', 'ctx'))
- grad_wouter: float32 [4096, 1024], P(('seq', 'ctx'))
- grad_bouter: float32 [1024], P(('seq', 'ctx'))
- grad_gffn: float32 [1024], P(('seq', 'ctx'))
- grad_sffn: float32 [1024], P(('seq', 'ctx'))
Inputs may be any that keep to these rules, and one draw needn't show every extreme that they name: `segments`: each row is one sequence. Segment numbers never fall, start at 0 and end at 2 in every row; segment 1 begins within the first 512 positions and ends within the last 512.
All inputs are finite; a program needn't handle non-finite values.
Results may differ from a plain program's by a relative error of at most 0.015.
Values may be sent and summed in bfloat16 or wider, within the bound.
A program may use at most 192 MiB of HBM per device.

v0:
```python
import jax
import jax.numpy as jnp
from jax import lax
from jax.sharding import PartitionSpec as P

HEAD_DIM = 64


def layer_norm(z, gain, shift):
    center = z - jnp.mean(z, axis=-1, keepdims=True)
    spread = jnp.mean(center * center, axis=-1, keepdims=True)
    return center * lax.rsqrt(spread + 1e-05) * gain + shift


def exact_gelu(value):
    return jax.nn.gelu(value, approximate=False)


def matmul_tn(left, right):
    return lax.dot_general(
        left, right, (((0,), (0,)), ((), ())), preferred_element_type=jnp.float32
    )


def matmul_nt(left, right):
    return lax.dot_general(
        left, right, (((1,), (1,)), ((), ())), preferred_element_type=jnp.float32
    )


def head_cols(array, head):
    return lax.dynamic_slice_in_dim(array, head * HEAD_DIM, HEAD_DIM, 1)


def join_heads(stacked):
    count, rows, size = stacked.shape
    return jnp.transpose(stacked, (1, 0, 2)).reshape(rows, count * size)


def owner_cols(gathered, position, seq_count, ctx_count):
    group_rows, columns = gathered.shape
    block = columns // (seq_count * ctx_count)
    shaped = gathered.reshape(group_rows, seq_count, ctx_count, block)
    picked = lax.dynamic_index_in_dim(shaped, position, 2, keepdims=False)
    return picked.reshape(group_rows, seq_count * block)


def per_device(
    tokens,
    segments,
    cotangent,
    w_query,
    b_query,
    w_key,
    w_value,
    b_value,
    w_output,
    b_output,
    gain_attn,
    shift_attn,
    w_inner,
    b_inner,
    w_outer,
    b_outer,
    gain_ffn,
    shift_ffn,
):
    f32 = jnp.float32
    bf16 = jnp.bfloat16
    attn_local = (
        w_query,
        w_key,
        w_value,
        w_output,
        b_query,
        b_value,
        b_output,
        gain_attn,
        shift_attn,
    )
    ffn_local = (w_inner, b_inner, w_outer, b_outer, gain_ffn, shift_ffn)
    attn_full = (
        lax.all_gather(attn_local[0], ("seq", "ctx"), axis=0, tiled=True),
        lax.all_gather(attn_local[1], ("seq", "ctx"), axis=0, tiled=True),
        lax.all_gather(attn_local[2], ("seq", "ctx"), axis=0, tiled=True),
        lax.all_gather(attn_local[3], ("seq", "ctx"), axis=0, tiled=True),
        lax.all_gather(attn_local[4], ("seq", "ctx"), axis=0, tiled=True),
        lax.all_gather(attn_local[5], ("seq", "ctx"), axis=0, tiled=True),
        lax.all_gather(attn_local[6], ("seq", "ctx"), axis=0, tiled=True),
        lax.all_gather(attn_local[7], ("seq", "ctx"), axis=0, tiled=True),
        lax.all_gather(attn_local[8], ("seq", "ctx"), axis=0, tiled=True),
    )
    ffn_full = (
        lax.all_gather(ffn_local[0], ("seq", "ctx"), axis=0, tiled=True),
        lax.all_gather(ffn_local[1], ("seq", "ctx"), axis=0, tiled=True),
        lax.all_gather(ffn_local[2], ("seq", "ctx"), axis=0, tiled=True),
        lax.all_gather(ffn_local[3], ("seq", "ctx"), axis=0, tiled=True),
        lax.all_gather(ffn_local[4], ("seq", "ctx"), axis=0, tiled=True),
        lax.all_gather(ffn_local[5], ("seq", "ctx"), axis=0, tiled=True),
    )
    wquery, wkey, wvalue, woutput, bquery, bvalue, boutput, gattn, sattn = attn_full
    winner, binner, wouter, bouter, gffn, sffn = ffn_full
    rows = tokens.shape[0]
    width = tokens.shape[1]
    heads = width // HEAD_DIM
    seq_count = lax.axis_size("seq")
    ctx_count = lax.axis_size("ctx")
    ctx_place = lax.axis_index("ctx")
    queries = (jnp.dot(tokens, wquery, preferred_element_type=f32) + bquery.astype(f32)).astype(
        bf16
    )
    keys_local = jnp.dot(tokens, wkey, preferred_element_type=f32).astype(bf16)
    values_local = (
        jnp.dot(tokens, wvalue, preferred_element_type=f32) + bvalue.astype(f32)
    ).astype(bf16)
    keys, values = (
        lax.all_gather(keys_local, "ctx", axis=0, tiled=True),
        lax.all_gather(values_local, "ctx", axis=0, tiled=True),
    )
    labels = segments[0]
    query_labels = lax.dynamic_slice_in_dim(labels, ctx_place * rows, rows, 0)
    allowed = query_labels[:, None] == labels[None, :]

    def scores_of(head):
        scaled = matmul_nt(head_cols(queries, head), head_cols(keys, head)) * 0.125
        return jnp.where(allowed, scaled, -1000000000.0)

    def forward_head(head):
        masked = scores_of(head)
        peak = jnp.max(masked, axis=-1, keepdims=True)
        expo = jnp.exp(masked - peak)
        total = jnp.sum(expo, axis=-1, keepdims=True)
        probs = (expo / total).astype(bf16)
        mixed = jnp.dot(probs, head_cols(values, head), preferred_element_type=f32)
        return (mixed, (peak + jnp.log(total))[:, 0])

    mixed_heads, logsum = lax.map(forward_head, jnp.arange(heads))
    attended = join_heads(mixed_heads).astype(bf16)
    pre_one = (
        tokens.astype(f32)
        + jnp.dot(attended, woutput, preferred_element_type=f32)
        + boutput.astype(f32)
    )
    normed_one = layer_norm(pre_one, gattn.astype(f32), sattn.astype(f32))
    normed_low = normed_one.astype(bf16)
    inner = jnp.dot(normed_low, winner, preferred_element_type=f32) + binner.astype(f32)
    act_low = exact_gelu(inner).astype(bf16)
    pre_two = normed_one + jnp.dot(act_low, wouter, preferred_element_type=f32) + bouter.astype(f32)
    out_value = layer_norm(pre_two, gffn.astype(f32), sffn.astype(f32))
    winner, binner, wouter, bouter, gffn, sffn = (
        lax.all_gather(ffn_local[0], ("seq", "ctx"), axis=0, tiled=True),
        lax.all_gather(ffn_local[1], ("seq", "ctx"), axis=0, tiled=True),
        lax.all_gather(ffn_local[2], ("seq", "ctx"), axis=0, tiled=True),
        lax.all_gather(ffn_local[3], ("seq", "ctx"), axis=0, tiled=True),
        lax.all_gather(ffn_local[4], ("seq", "ctx"), axis=0, tiled=True),
        lax.all_gather(ffn_local[5], ("seq", "ctx"), axis=0, tiled=True),
    )
    grad_out = cotangent.astype(f32)
    unused, norm_two_back = jax.vjp(layer_norm, pre_two, gffn.astype(f32), sffn.astype(f32))
    d_pre_two, d_gain_two, d_shift_two = norm_two_back(grad_out)
    outer_low = d_pre_two.astype(bf16)
    grad_bouter = jnp.sum(outer_low.astype(f32), axis=0)
    d_act = matmul_nt(outer_low, wouter)
    unused_act, gelu_back = jax.vjp(exact_gelu, inner)
    d_inner = gelu_back(d_act)[0]
    inner_low = d_inner.astype(bf16)
    grad_binner = jnp.sum(inner_low.astype(f32), axis=0)
    d_normed = d_pre_two + matmul_nt(inner_low, winner)
    group_normed, group_act, group_outer, group_inner = (
        lax.all_gather(normed_low, "ctx", axis=0, tiled=True),
        lax.all_gather(act_low, "ctx", axis=0, tiled=True),
        lax.all_gather(outer_low, "ctx", axis=0, tiled=True),
        lax.all_gather(inner_low, "ctx", axis=0, tiled=True),
    )
    part_winner = matmul_tn(owner_cols(group_normed, ctx_place, seq_count, ctx_count), group_inner)
    part_wouter = matmul_tn(owner_cols(group_act, ctx_place, seq_count, ctx_count), group_outer)
    out_winner, out_wouter = (
        lax.psum_scatter(part_winner, "seq", scatter_dimension=0, tiled=True),
        lax.psum_scatter(part_wouter, "seq", scatter_dimension=0, tiled=True),
    )
    wquery, wkey, wvalue, woutput, bquery, bvalue, boutput, gattn, sattn = (
        lax.all_gather(attn_local[0], ("seq", "ctx"), axis=0, tiled=True),
        lax.all_gather(attn_local[1], ("seq", "ctx"), axis=0, tiled=True),
        lax.all_gather(attn_local[2], ("seq", "ctx"), axis=0, tiled=True),
        lax.all_gather(attn_local[3], ("seq", "ctx"), axis=0, tiled=True),
        lax.all_gather(attn_local[4], ("seq", "ctx"), axis=0, tiled=True),
        lax.all_gather(attn_local[5], ("seq", "ctx"), axis=0, tiled=True),
        lax.all_gather(attn_local[6], ("seq", "ctx"), axis=0, tiled=True),
        lax.all_gather(attn_local[7], ("seq", "ctx"), axis=0, tiled=True),
        lax.all_gather(attn_local[8], ("seq", "ctx"), axis=0, tiled=True),
    )
    unused_one, norm_one_back = jax.vjp(layer_norm, pre_one, gattn.astype(f32), sattn.astype(f32))
    d_pre_one, d_gain_one, d_shift_one = norm_one_back(d_normed)
    out_low = d_pre_one.astype(bf16)
    grad_boutput = jnp.sum(out_low.astype(f32), axis=0)
    d_attended = matmul_nt(out_low, woutput).astype(bf16)

    def backward_head(item):
        head, head_lse = item
        probs = jnp.exp(scores_of(head) - head_lse[:, None])
        d_mixed = head_cols(d_attended, head)
        value_cols = head_cols(values, head)
        d_probs = matmul_nt(d_mixed, value_cols)
        d_scores = probs * (d_probs - jnp.sum(d_probs * probs, axis=-1, keepdims=True))
        scores_low = d_scores.astype(bf16)
        d_query = jnp.dot(scores_low, head_cols(keys, head), preferred_element_type=f32) * 0.125
        d_key = matmul_tn(scores_low, head_cols(queries, head)) * 0.125
        d_value = matmul_tn(probs.astype(bf16), d_mixed)
        return (d_query, d_key, d_value)

    query_heads, key_heads, value_heads = lax.map(backward_head, (jnp.arange(heads), logsum))
    query_low = join_heads(query_heads).astype(bf16)
    key_sum, value_sum = (
        lax.psum_scatter(join_heads(key_heads), "ctx", scatter_dimension=0, tiled=True),
        lax.psum_scatter(join_heads(value_heads), "ctx", scatter_dimension=0, tiled=True),
    )
    key_low = key_sum.astype(bf16)
    value_low = value_sum.astype(bf16)
    grad_bquery = jnp.sum(query_low.astype(f32), axis=0)
    grad_bvalue = jnp.sum(value_low.astype(f32), axis=0)
    grad_tokens = (
        d_pre_one
        + matmul_nt(query_low, wquery)
        + matmul_nt(key_low, wkey)
        + matmul_nt(value_low, wvalue)
    )
    group_tokens, group_attended, group_out, group_query, group_key, group_value = (
        lax.all_gather(tokens, "ctx", axis=0, tiled=True),
        lax.all_gather(attended, "ctx", axis=0, tiled=True),
        lax.all_gather(out_low, "ctx", axis=0, tiled=True),
        lax.all_gather(query_low, "ctx", axis=0, tiled=True),
        lax.all_gather(key_low, "ctx", axis=0, tiled=True),
        lax.all_gather(value_low, "ctx", axis=0, tiled=True),
    )
    own_tokens = owner_cols(group_tokens, ctx_place, seq_count, ctx_count)
    own_attended = owner_cols(group_attended, ctx_place, seq_count, ctx_count)
    part_wquery = matmul_tn(own_tokens, group_query)
    part_wkey = matmul_tn(own_tokens, group_key)
    part_wvalue = matmul_tn(own_tokens, group_value)
    part_woutput = matmul_tn(own_attended, group_out)
    out_wquery, out_wkey, out_wvalue, out_woutput = (
        lax.psum_scatter(part_wquery, "seq", scatter_dimension=0, tiled=True),
        lax.psum_scatter(part_wkey, "seq", scatter_dimension=0, tiled=True),
        lax.psum_scatter(part_wvalue, "seq", scatter_dimension=0, tiled=True),
        lax.psum_scatter(part_woutput, "seq", scatter_dimension=0, tiled=True),
    )
    vector_sums = (
        lax.psum_scatter(grad_bquery, ("seq", "ctx"), scatter_dimension=0, tiled=True),
        lax.psum_scatter(grad_bvalue, ("seq", "ctx"), scatter_dimension=0, tiled=True),
        lax.psum_scatter(grad_boutput, ("seq", "ctx"), scatter_dimension=0, tiled=True),
        lax.psum_scatter(d_gain_one, ("seq", "ctx"), scatter_dimension=0, tiled=True),
        lax.psum_scatter(d_shift_one, ("seq", "ctx"), scatter_dimension=0, tiled=True),
        lax.psum_scatter(grad_binner, ("seq", "ctx"), scatter_dimension=0, tiled=True),
        lax.psum_scatter(grad_bouter, ("seq", "ctx"), scatter_dimension=0, tiled=True),
        lax.psum_scatter(d_gain_two, ("seq", "ctx"), scatter_dimension=0, tiled=True),
        lax.psum_scatter(d_shift_two, ("seq", "ctx"), scatter_dimension=0, tiled=True),
    )
    (
        out_bquery,
        out_bvalue,
        out_boutput,
        out_gattn,
        out_sattn,
        out_binner,
        out_bouter,
        out_gffn,
        out_sffn,
    ) = vector_sums
    return (
        out_value.astype(bf16),
        grad_tokens,
        out_wquery,
        out_bquery,
        out_wkey,
        out_wvalue,
        out_bvalue,
        out_woutput,
        out_boutput,
        out_gattn,
        out_sattn,
        out_winner,
        out_binner,
        out_wouter,
        out_bouter,
        out_gffn,
        out_sffn,
    )


def solution(mesh):
    return jax.shard_map(
        per_device,
        mesh=mesh,
        in_specs=(
            P(("seq", "ctx"), None),
            P("seq", None),
            P(("seq", "ctx"), None),
            P(("seq", "ctx"), None),
            P(("seq", "ctx")),
            P(("seq", "ctx"), None),
            P(("seq", "ctx"), None),
            P(("seq", "ctx")),
            P(("seq", "ctx"), None),
            P(("seq", "ctx")),
            P(("seq", "ctx")),
            P(("seq", "ctx")),
            P(("seq", "ctx"), None),
            P(("seq", "ctx")),
            P(("seq", "ctx"), None),
            P(("seq", "ctx")),
            P(("seq", "ctx")),
            P(("seq", "ctx")),
        ),
        out_specs=(
            P(("seq", "ctx"), None),
            P(("seq", "ctx"), None),
            P(("seq", "ctx"), None),
            P(("seq", "ctx")),
            P(("seq", "ctx"), None),
            P(("seq", "ctx"), None),
            P(("seq", "ctx")),
            P(("seq", "ctx"), None),
            P(("seq", "ctx")),
            P(("seq", "ctx")),
            P(("seq", "ctx")),
            P(("seq", "ctx"), None),
            P(("seq", "ctx")),
            P(("seq", "ctx"), None),
            P(("seq", "ctx")),
            P(("seq", "ctx")),
            P(("seq", "ctx")),
        ),
        check_vma=False,
    )
```

profile of v0, /device:TPU:0, one launch (start us, length us, event | category | flops | bytes accessed | tf_op | source)
XLA Modules:
  0.0 1753.7 jit_solution(10190511337416466784)
XLA Ops:
  16.2 42.2 %all-reduce.18 = (bf16[1024]{0:T(1024)(128)(2,1)S(1)}, bf16[1024]{0:T(1024)(128)(2,1)S(1)}, bf16[1024]{0:T(1024)(128)(2,1)S(1)}, bf16[1024]{0:T(1024)(128)(2,1)S...) all-reduce(bf16[1024]{0:T(1024)(128)(2,1)S(1)} %dynamic-update-slic, ...), channel_id=1, replica_groups=mesh['seq'=16,'ctx'=2] {'seq','ctx'}, use_global_device_ids=true, to_apply=%add | all-reduce | flops 8192 | bytes 32768
  58.4 12.0 all-gather.26.cloned.1.call-done
  70.4 4.1 add_convert_fusion.2
  74.6 54.4 %all-gather.22.cloned.1.call-done = bf16[1024,1024]{1,0:T(8,128)(2,1)} async-done(((bf16[32,1024]{1,0:T(8,128)(2,1)}), bf16[1024,1024]{1,0:T(8,128)(2,1)}) %all-gather.22.cloned.1.call-update) | async-done | bytes 2097168 | tf_op jit(solution)/shard_map/all_gather | solution.py:84
  129.0 3.8 convolution_convert_fusion.1
  135.1 66.1 %all-gather = bf16[32,1,128]{2,1,0:T(2,128)(2,1)S(1)} all-gather(bf16[1,1,128]{2,1,0:T(2,128)(2,1)S(1)} %bitcast.122), channel_id=1, replica_groups=mesh['seq'=16,'ctx'=2] {'seq','ctx'}, dimensions={0}, use_global_device_ids=true | all-gather | bytes 8448 | tf_op jit(solution)/shard_map/all_gather | solution.py:95
  201.3 3.8 add_convert_fusion.3
  205.1 16.4 all-gather.28.cloned.1.call-done
  221.6 35.1 %all-gather.24.cloned.1.call-done = bf16[1024,1024]{1,0:T(8,128)(2,1)} async-done(((bf16[512,1024]{1,0:T(8,128)(2,1)}), bf16[1024,1024]{1,0:T(8,128)(2,1)}) %all-gather.24.cloned.1.call-update) | async-done | bytes 2097168 | tf_op jit(solution)/shard_map/all_gather | solution.py:117
  256.8 81.9 %while.28 = (s32[]{:T(128)}, bf16[16,512,64]{1,2,0:T(8,128)(2,1)S(1)}, f32[16,512]{1,0:T(8,128)S(1)}, s32[16]{0:T(128)S(1)}, bf16[512,1024]{1,0:T(8,128)(2,1)}, ...) while((s32[]{:T(128)}, ...), condition=%wide.region_3.4_spmd.clone, body=%wide.region_0.3_spmd.clone.sunk | while | flops 138935808 | bytes 7106239 | solution.py:137
  338.7 3.6 fusion.48
  343.1 52.5 %all-gather.32.cloned.1.call-done = bf16[1024,4096]{1,0:T(8,128)(2,1)} async-done(((bf16[32,4096]{1,0:T(8,128)(2,1)}), bf16[1024,4096]{1,0:T(8,128)(2,1)}) %all-gather.32.cloned.1.call-update) | async-done | bytes 8388624 | tf_op jit(solution)/shard_map/all_gather | solution.py:94
  395.6 26.0 %multiply_convert_fusion.1 = (bf16[512,4096]{1,0:T(8,128)(2,1)}, f32[512,4096]{1,0:T(8,128)}, f32[512,4096]{1,0:T(8,128)}) fusion(f32[4096]{0:T(1024)S(1)} %bitcast.118, bf16[512,1024]{1,0:T(8,128)(2,1)S(1)} %fusion.41, bf16[1024,4096]{1,0:T(8,128)(2,1)} %all-gather.32.cloned.1.call-done), kind=kOutput, calls=%fused_computation.45 | convolution fusion | flops 4433379328 | bytes 30425088 | tf_op jit(solution)/shard_map/dot_general | solution.py:146
  421.6 53.0 %all-gather.34.cloned.1.call-done = bf16[4096,1024]{1,0:T(8,128)(2,1)} async-done(((bf16[128,1024]{1,0:T(8,128)(2,1)}), bf16[4096,1024]{1,0:T(8,128)(2,1)}) %all-gather.34.cloned.1.call-update) | async-done | bytes 8388624 | tf_op jit(solution)/shard_map/all_gather | solution.py:96
  474.6 8.9 fusion.49
  489.0 15.1 convert_reduce_fusion
  504.1 10.3 multiply_reduce_fusion.1
  516.8 3.3 convolution_convert_fusion
  520.2 150.3 %while.29 = (s32[]{:T(128)}, bf16[16,512,64]{1,2,0:T(8,128)(2,1)S(1)}, f32[16,1024,64]{1,2,0:T(8,128)}, f32[16,1024,64]{1,2,0:T(8,128)}, s32[16]{0:T(128)S(1)}, ...) while((s32[]{:T(128)}, ...), condition=%wide.region_14.15_spmd.clone, body=%wide.region_12.14_spmd.clone.sunk | while | flops 340884992 | bytes 17714912 | solution.py:211
  525.0 2.0 fusion.124
  534.4 2.0 fusion.124
  543.8 2.0 fusion.124
  553.2 2.0 fusion.124
  562.6 2.0 fusion.124
  572.0 2.0 fusion.124
  581.4 2.0 fusion.124
  590.8 2.0 fusion.124
  600.2 2.0 fusion.124
  609.5 2.0 fusion.124
  628.3 2.0 fusion.124
  637.7 2.0 fusion.124
  665.9 2.0 fusion.124
  676.0 47.5 %reduce-scatter.11.cloned.1.call-done = f32[512,1024]{0,1:T(8,128)} async-done(((f32[1024,1024]{0,1:T(8,128)}), f32[512,1024]{0,1:T(8,128)}) %reduce-scatter.11.cloned.1.call-update) | async-done | bytes 2097168 | tf_op jit(solution)/shard_map/reduce_scatter | solution.py:215
  723.6 2.7 convert_reduce_fusion.4
  726.3 53.8 %reduce-scatter.9.cloned.1.call-done = f32[512,1024]{0,1:T(8,128)} async-done(((f32[1024,1024]{0,1:T(8,128)}), f32[512,1024]{0,1:T(8,128)}) %reduce-scatter.9.cloned.1.call-update) | async-done | bytes 2097168 | tf_op jit(solution)/shard_map/reduce_scatter | solution.py:214
  780.2 2.8 convert_element_type.144
  785.5 29.4 %all-gather.36.cloned.1.call-done = bf16[1024,1024]{0,1:T(8,128)(2,1)} async-done(((bf16[512,1024]{0,1:T(8,128)(2,1)}), bf16[1024,1024]{0,1:T(8,128)(2,1)}) %all-gather.36.cloned.1.call-update) | async-done | bytes 2097168 | tf_op jit(solution)/shard_map/all_gather | solution.py:228
  816.2 33.8 %all-gather.38.cloned.1.call-done = bf16[1024,1024]{0,1:T(8,128)(2,1)} async-done(((bf16[512,1024]{0,1:T(8,128)(2,1)}), bf16[1024,1024]{0,1:T(8,128)(2,1)}) %all-gather.38.cloned.1.call-update) | async-done | bytes 2097168 | tf_op jit(solution)/shard_map/all_gather | solution.py:231
  850.0 4.2 fusion.52
  854.5 30.2 %all-gather.44.cloned.1.call-done = bf16[1024,1024]{0,1:T(8,128)(2,1)} async-done(((bf16[512,1024]{0,1:T(8,128)(2,1)}), bf16[1024,1024]{0,1:T(8,128)(2,1)}) %all-gather.44.cloned.1.call-update) | async-done | bytes 2097168 | tf_op jit(solution)/shard_map/all_gather | solution.py:229
  886.0 33.2 %all-gather.46.cloned.1.call-done = bf16[1024,1024]{1,0:T(8,128)(2,1)} async-done(((bf16[512,1024]{1,0:T(8,128)(2,1)}), bf16[1024,1024]{1,0:T(8,128)(2,1)}) %all-gather.46.cloned.1.call-update) | async-done | bytes 2097168 | tf_op jit(solution)/shard_map/all_gather | solution.py:230
  919.3 4.2 fusion.55
  923.5 30.3 %all-gather.42.cloned.1.call-done = bf16[1024,1024]{0,1:T(8,128)(2,1)} async-done(((bf16[512,1024]{0,1:T(8,128)(2,1)}), bf16[1024,1024]{0,1:T(8,128)(2,1)}) %all-gather.42.cloned.1.call-update) | async-done | bytes 2097168 | tf_op jit(solution)/shard_map/all_gather | solution.py:233
  953.8 4.2 fusion.54
  958.1 30.3 %all-gather.40.cloned.1.call-done = bf16[1024,1024]{0,1:T(8,128)(2,1)} async-done(((bf16[512,1024]{0,1:T(8,128)(2,1)}), bf16[1024,1024]{0,1:T(8,128)(2,1)}) %all-gather.40.cloned.1.call-update) | async-done | bytes 2097168 | tf_op jit(solution)/shard_map/all_gather | solution.py:232
  988.3 4.2 fusion.53
  992.6 101.2 %all-gather.52.cloned.1.call-done = bf16[1024,4096]{1,0:T(8,128)(2,1)} async-done(((bf16[512,4096]{1,0:T(8,128)(2,1)}), bf16[1024,4096]{1,0:T(8,128)(2,1)}) %all-gather.52.cloned.1.call-update) | async-done | bytes 8388624 | tf_op jit(solution)/shard_map/all_gather | solution.py:171
  1093.8 14.5 reshape.183
  1108.3 10.9 constant_dynamic-slice_fusion.1
  1119.2 20.0 %copy.41 = bf16[1024,16,1,128]{0,3,1,2:T(8,128)(2,1)} copy(bf16[1024,16,1,128]{3,2,1,0:T(2,128)(2,1)} %constant_dynamic-slice_fusion.1) | data formatting | bytes 8388608
  1139.2 10.7 fusion.57
  1150.1 12.9 all-gather.48.cloned.1.call-done
  1163.0 2.9 copy.39
  1166.0 102.5 %all-gather.50.cloned.1.call-done = bf16[1024,4096]{1,0:T(8,128)(2,1)} async-done(((bf16[512,4096]{1,0:T(8,128)(2,1)}), bf16[1024,4096]{1,0:T(8,128)(2,1)}) %all-gather.50.cloned.1.call-update) | async-done | bytes 8388624 | tf_op jit(solution)/shard_map/all_gather | solution.py:173
  1268.5 10.1 fusion.56
  1280.1 4.3 fusion.50
  1284.4 40.8 %all-reduce.17 = (f32[1024]{0:T(1024)S(1)}, f32[1024]{0:T(1024)S(1)}, f32[1024]{0:T(1024)S(1)}, f32[1024]{0:T(1024)S(1)}, f32[1024]{0:T(1024)S(1)}, /*index=5*/f...) all-reduce(f32[1024]{0:T(1024)S(1)} %reduce_sum.185, ...), channel_id=5, replica_groups=mesh['seq'=16,'ctx'=2] {'seq','ctx'}, use_global_device_ids=true, to_apply=%region_19.20.clone | all-reduce | flops 12288 | bytes 98304
  1330.5 3.0 fusion.51
  1334.3 2.9 add_add_fusion.2
  1337.2 62.5 %reduce-scatter.19.cloned.1.call-done = f32[32,1024]{1,0:T(8,128)} async-done(((f32[512,1024]{1,0:T(8,128)}), f32[32,1024]{1,0:T(8,128)}) %reduce-scatter.19.cloned.1.call-update) | async-done | bytes 131088 | tf_op jit(solution)/shard_map/reduce_scatter | solution.py:245
  1399.7 64.9 %reduce-scatter.17.cloned.1.call-done = f32[32,1024]{1,0:T(8,128)} async-done(((f32[512,1024]{1,0:T(8,128)}), f32[32,1024]{1,0:T(8,128)}) %reduce-scatter.17.cloned.1.call-update) | async-done | bytes 131088 | tf_op jit(solution)/shard_map/reduce_scatter | solution.py:244
  1464.6 65.2 %reduce-scatter.15.cloned.1.call-done = f32[32,1024]{1,0:T(8,128)} async-done(((f32[512,1024]{1,0:T(8,128)}), f32[32,1024]{1,0:T(8,128)}) %reduce-scatter.15.cloned.1.call-update) | async-done | bytes 131088 | tf_op jit(solution)/shard_map/reduce_scatter | solution.py:243
  1529.8 108.2 %reduce-scatter.23.cloned.1.call-done = f32[128,1024]{1,0:T(8,128)} async-done(((f32[2048,1024]{1,0:T(8,128)}), f32[128,1024]{1,0:T(8,128)}) %reduce-scatter.23.cloned.1.call-update) | async-done | bytes 524304 | tf_op jit(solution)/shard_map/reduce_scatter | solution.py:179
  1638.0 108.9 %reduce-scatter.21.cloned.1.call-done = f32[32,4096]{1,0:T(8,128)} async-done(((f32[512,4096]{1,0:T(8,128)}), f32[32,4096]{1,0:T(8,128)}) %reduce-scatter.21.cloned.1.call-update) | async-done | bytes 524304 | tf_op jit(solution)/shard_map/reduce_scatter | solution.py:178
  (367 shorter events, 222.9 us)
Async XLA Ops:
  7.2 63.2 %all-gather.26.cloned.1.call-start = ((), (), s32[]{:S(2)}) async-start(), calls=%async_computation.11 | async-start | bytes 2162688 | tf_op jit(solution)/shard_map/all_gather | solution.py:85
  7.9 121.1 %all-gather.22.cloned.1.call-start = ((), (), s32[]{:S(2)}) async-start(), calls=%async_computation.9 | async-start | bytes 2162688 | tf_op jit(solution)/shard_map/all_gather | solution.py:84
  8.7 192.6 %all-gather.20.cloned.1.call-start = ((), (), s32[]{:S(2)}) async-start(), calls=%async_computation.8 | async-start | bytes 2162688 | tf_op jit(solution)/shard_map/all_gather | solution.py:83
  9.4 212.2 %all-gather.28.cloned.1.call-start = ((), (), s32[]{:S(2)}) async-start(), calls=%async_computation.12 | async-start | bytes 3145728 | tf_op jit(solution)/shard_map/all_gather | solution.py:118
  58.4 70.6 %copy-start.11 = (bf16[512,1024]{1,0:T(8,128)(2,1)S(1)}, bf16[512,1024]{1,0:T(8,128)(2,1)}, u32[]{:S(2)}) copy-start(bf16[512,1024]{1,0:T(8,128)(2,1)} %param.22) | copy-start | bytes 3145732
  74.5 60.5 %copy-start.17 = (bf16[128]{0:T(256)(128)(2,1)S(1)}, bf16[128]{0:T(256)(128)(2,1)}, u32[]{:S(2)}) copy-start(bf16[128]{0:T(256)(128)(2,1)} %param.35) | copy-start | bytes 772
  74.5 126.7 %copy-start.16 = (s32[1,1024]{1,0:T(1,128)S(1)}, s32[1,1024]{1,0:T(1,128)}, u32[]{:S(2)}) copy-start(s32[1,1024]{1,0:T(1,128)} %param.23) | copy-start | bytes 12292
  74.6 182.1 %all-gather.24.cloned.1.call-start = ((), (), s32[]{:S(2)}) async-start(), calls=%async_computation.10 | async-start | bytes 3145728 | tf_op jit(solution)/shard_map/all_gather | solution.py:117
  132.9 205.8 %all-gather.30.cloned.1.call-start = ((), (), s32[]{:S(2)}) async-start(), calls=%async_computation.13 | async-start | bytes 2162688 | tf_op jit(solution)/shard_map/all_gather | solution.py:86
  133.4 262.1 %all-gather.32.cloned.1.call-start = ((), (), s32[]{:S(2)}) async-start(), calls=%async_computation.14 | async-start | bytes 8650752 | tf_op jit(solution)/shard_map/all_gather | solution.py:94
  134.2 340.4 %all-gather.34.cloned.1.call-start = ((), (), s32[]{:S(2)}) async-start(), calls=%async_computation.15 | async-start | bytes 8650752 | tf_op jit(solution)/shard_map/all_gather | solution.py:96
  134.9 588.6 %reduce-scatter.11.cloned.1.call-start = ((), (), s32[]{:S(2)}) async-start(), calls=%async_computation.17 | async-start | bytes 6291456 | tf_op jit(solution)/shard_map/reduce_scatter | solution.py:215
  338.7 3.6 copy-start.5
  343.1 78.5 %copy-start.8 = (bf16[512,1024]{1,0:T(8,128)(2,1)}, bf16[512,1024]{1,0:T(8,128)(2,1)S(1)}, u32[]{:S(2)}) copy-start(bf16[512,1024]{1,0:T(8,128)(2,1)S(1)} %fusion.41) | copy-start | bytes 3145732
  483.5 1.2 copy-start.13
  487.5 1.3 copy-start.6
  489.0 15.1 copy-start.9
  515.1 1.4 copy-start
  516.8 3.3 copy-start.10
  670.5 1.0 copy-start.3
  671.5 108.7 %reduce-scatter.9.cloned.1.call-start = ((), (), s32[]{:S(2)}) async-start(), calls=%async_computation.16 | async-start | bytes 6291456 | tf_op jit(solution)/shard_map/reduce_scatter | solution.py:214
  671.5 1.2 copy-start.12
  672.0 142.8 %all-gather.36.cloned.1.call-start = ((), (), s32[]{:S(2)}) async-start(), calls=%async_computation.18 | async-start | bytes 3145728 | tf_op jit(solution)/shard_map/all_gather | solution.py:228
  674.1 175.9 %all-gather.38.cloned.1.call-start = ((), (), s32[]{:S(2)}) async-start(), calls=%async_computation.19 | async-start | bytes 3145728 | tf_op jit(solution)/shard_map/all_gather | solution.py:231
  674.7 210.0 %all-gather.44.cloned.1.call-start = ((), (), s32[]{:S(2)}) async-start(), calls=%async_computation.25 | async-start | bytes 3145728 | tf_op jit(solution)/shard_map/all_gather | solution.py:229
  675.4 243.8 %all-gather.46.cloned.1.call-start = ((), (), s32[]{:S(2)}) async-start(), calls=%async_computation.26 | async-start | bytes 3145728 | tf_op jit(solution)/shard_map/all_gather | solution.py:230
  676.0 277.8 %all-gather.42.cloned.1.call-start = ((), (), s32[]{:S(2)}) async-start(), calls=%async_computation.23 | async-start | bytes 3145728 | tf_op jit(solution)/shard_map/all_gather | solution.py:233
  726.3 262.1 %all-gather.40.cloned.1.call-start = ((), (), s32[]{:S(2)}) async-start(), calls=%async_computation.21 | async-start | bytes 3145728 | tf_op jit(solution)/shard_map/all_gather | solution.py:232
  783.0 310.8 %all-gather.52.cloned.1.call-start = ((), (), s32[]{:S(2)}) async-start(), calls=%async_computation.31 | async-start | bytes 12582912 | tf_op jit(solution)/shard_map/all_gather | solution.py:171
  783.6 355.6 %all-gather.54.cloned.1.call-start = ((), (), s32[]{:S(2)}) async-start(), calls=%async_computation.32 | async-start | bytes 3145728 | tf_op jit(solution)/shard_map/all_gather | solution.py:172
  784.1 378.9 %all-gather.48.cloned.1.call-start = ((), (), s32[]{:S(2)}) async-start(), calls=%async_computation.28 | async-start | bytes 3145728 | tf_op jit(solution)/shard_map/all_gather | solution.py:170
  784.9 483.6 %all-gather.50.cloned.1.call-start = ((), (), s32[]{:S(2)}) async-start(), calls=%async_computation.29 | async-start | bytes 12582912 | tf_op jit(solution)/shard_map/all_gather | solution.py:173
  785.5 551.7 %reduce-scatter.13.cloned.1.call-start = ((), (), s32[]{:S(2)}) async-start(), calls=%async_computation.20 | async-start | bytes 2228224 | tf_op jit(solution)/shard_map/reduce_scatter | solution.py:242
  854.2 545.4 %reduce-scatter.19.cloned.1.call-start = ((), (), s32[]{:S(2)}) async-start(), calls=%async_computation.27 | async-start | bytes 2228224 | tf_op jit(solution)/shard_map/reduce_scatter | solution.py:245
  923.4 541.1 %reduce-scatter.17.cloned.1.call-start = ((), (), s32[]{:S(2)}) async-start(), calls=%async_computation.24 | async-start | bytes 2228224 | tf_op jit(solution)/shard_map/reduce_scatter | solution.py:244
  958.0 571.7 %reduce-scatter.15.cloned.1.call-start = ((), (), s32[]{:S(2)}) async-start(), calls=%async_computation.22 | async-start | bytes 2228224 | tf_op jit(solution)/shard_map/reduce_scatter | solution.py:243
  992.6 645.4 %reduce-scatter.23.cloned.1.call-start = ((), (), s32[]{:S(2)}) async-start(), calls=%async_computation.33 | async-start | bytes 8912896 | tf_op jit(solution)/shard_map/reduce_scatter | solution.py:179
  1149.9 597.0 %reduce-scatter.21.cloned.1.call-start = ((), (), s32[]{:S(2)}) async-start(), calls=%async_computation.30 | async-start | bytes 8912896 | tf_op jit(solution)/shard_map/reduce_scatter | solution.py:178
  1278.5 1.2 copy-start.4
  1280.0 50.4 %copy-start.7 = (bf16[512,1024]{0,1:T(8,128)(2,1)S(1)}, bf16[512,1024]{0,1:T(8,128)(2,1)}, u32[]{:S(2)}) copy-start(bf16[512,1024]{0,1:T(8,128)(2,1)} %convert_element_type.144) | copy-start | bytes 3145732
  1330.5 3.1 copy-start.1
  1330.5 3.1 copy-start.2
  1330.5 3.2 copy-start.14
  1330.5 3.8 copy-start.15
Sparse Core Ops, SparseCore 0:
  11.1 59.2 all-gather.25
  73.5 55.5 all-gather.21
  132.1 55.4 all-gather.19
  189.6 31.9 all-gather.27
  223.5 33.1 all-gather.23
  259.6 56.5 all-gather.29
  319.3 76.2 all-gather.31
  398.7 75.8 all-gather.33
  670.7 52.8 reduce-scatter.10
  725.8 54.3 reduce-scatter.8
  781.7 33.1 all-gather.35
  816.9 33.1 all-gather.37
  851.5 33.1 all-gather.43
  886.1 33.1 all-gather.45
  920.6 33.1 all-gather.41
  955.2 33.1 all-gather.39
  989.7 103.9 all-gather.51
  1095.2 33.1 all-gather.53
  1129.9 33.1 all-gather.47
  1164.4 103.9 all-gather.49
  1272.8 61.4 reduce-scatter.12
  1339.0 60.6 reduce-scatter.18
  1404.0 60.5 reduce-scatter.16
  1469.2 60.5 reduce-scatter.14
  1534.4 103.5 reduce-scatter.22
  1642.5 104.3 reduce-scatter.20
where the time goes:
time: 1760 us; the launch traced here: 1750 us
  waiting for transfers between devices  1150 us (65%)
  matrix products  305 us (17%)
  blocking collectives  149 us (8%)
  local copies, waits for them, and re-layouts  91.6 us (5%)
  other arithmetic  22.6 us (1%)
  loops' own time  22 us (1%)
    dot_general x54, matrix products, matmul_nt(): lax.dot_general(left, right, (((1,), (1,)), ((), ())), preferred_element_...  117 us
    reduce_scatter x1, waiting for transfers between devices, per_device(): lax.psum_scatter(part_winner, 'seq', scatter_dimension=0, tiled=True)  109 us
    reduce_scatter x1, waiting for transfers between devices, per_device(): lax.psum_scatter(part_wouter, 'seq', scatter_dimension=0, tiled=True)  108 us
    all_gather x1, waiting for transfers between devices, per_device(): lax.all_gather(inner_low, 'ctx', axis=0, tiled=True)  102 us
    all_gather x1, waiting for transfers between devices, per_device(): lax.all_gather(act_low, 'ctx', axis=0, tiled=True)  101 us
    dot_general x38, matrix products, matmul_tn(): lax.dot_general(left, right, (((0,), (0,)), ((), ())), preferred_element_...  87.6 us
    unnamed x2, blocking collectives  83.1 us
    all_gather x1, blocking collectives, per_device(): lax.all_gather(ffn_local[1], ('seq', 'ctx'), axis=0, tiled=True)  66.1 us
  transfers between devices with their start and end apart: 26, of which 22 were waited for; matrix products, arithmetic and copies ran while one was open for 13% of the time, Pallas kernels for 0%

commit v1 on v0

v1 whole, which is shorter than its diff:
```python
import functools

import jax
import jax.numpy as jnp
from jax import lax
from jax.experimental import pallas as pl
from jax.experimental.pallas import tpu as pltpu
from jax.sharding import PartitionSpec as P

HEAD_DIM = 64
BOTH = ("seq", "ctx")
F32 = jnp.float32
BF16 = jnp.bfloat16


def layer_norm(z, gain, shift):
    center = z - jnp.mean(z, axis=-1, keepdims=True)
    spread = jnp.mean(center * center, axis=-1, keepdims=True)
    return center * lax.rsqrt(spread + 1e-05) * gain + shift


def exact_gelu(value):
    return jax.nn.gelu(value, approximate=False)


def matmul_tn(left, right):
    return lax.dot_general(
        left, right, (((0,), (0,)), ((), ())), preferred_element_type=F32
    )


def matmul_nt(left, right):
    return lax.dot_general(
        left, right, (((1,), (1,)), ((), ())), preferred_element_type=F32
    )


def head_part(array, index):
    lane = lax.broadcasted_iota(jnp.int32, array.shape, 1)
    inside = (lane >= index * HEAD_DIM) & (lane < (index + 1) * HEAD_DIM)
    return jnp.where(inside, array, jnp.zeros_like(array))


def probs_of(queries, keys, allowed):
    masked = jnp.where(allowed, matmul_nt(queries, keys), -1000000000.0)
    expo = jnp.exp(masked - jnp.max(masked, axis=-1, keepdims=True))
    return expo * (1.0 / jnp.sum(expo, axis=-1, keepdims=True))


def attend_kernel(q_ref, k_ref, v_ref, col_ref, row_ref, out_ref):
    allowed = col_ref[...] == row_ref[...]
    queries = q_ref[...] * jnp.asarray(0.125, BF16)
    total = jnp.zeros(out_ref.shape, F32)
    for index in range(2):
        probs = probs_of(queries, head_part(k_ref[...], index), allowed).astype(BF16)
        total += jnp.dot(probs, head_part(v_ref[...], index), preferred_element_type=F32)
    out_ref[...] = total.astype(BF16)


def attend_back_kernel(
    q_ref, k_ref, v_ref, g_ref, col_ref, row_ref, dq_ref, dk_ref, dv_ref, dk_sum, dv_sum
):
    step = pl.program_id(1)
    allowed = col_ref[...] == row_ref[...]
    queries = q_ref[...] * jnp.asarray(0.125, BF16)
    grads = g_ref[...]

    @pl.when(step == 0)
    def _():
        dk_sum[...] = jnp.zeros_like(dk_sum)
        dv_sum[...] = jnp.zeros_like(dv_sum)

    dq = jnp.zeros(dq_ref.shape, F32)
    for index in range(2):
        keys = head_part(k_ref[...], index)
        probs = probs_of(queries, keys, allowed)
        d_probs = matmul_nt(grads, head_part(v_ref[...], index))
        inner = jnp.sum(d_probs * probs, axis=-1, keepdims=True)
        scores_low = (probs * (d_probs - inner)).astype(BF16)
        dq += jnp.dot(scores_low, keys, preferred_element_type=F32)
        dk_sum[...] += matmul_tn(scores_low, head_part(queries, index))
        dv_sum[...] += matmul_tn(probs.astype(BF16), head_part(grads, index))
    dq_ref[...] = (dq * 0.125).astype(BF16)

    @pl.when(step == pl.num_programs(1) - 1)
    def _():
        dk_ref[...] = dk_sum[...].astype(BF16)
        dv_ref[...] = dv_sum[...].astype(BF16)


def attention_specs(length, pairs, block):
    rows = pl.BlockSpec((block, 128), lambda p, i: (i, p))

    def whole(third):
        return pl.BlockSpec((length, 128), lambda p, i: (0, p + third * pairs))

    labels = [
        pl.BlockSpec((block, 1), lambda p, i: (i, 0)),
        pl.BlockSpec((1, length), lambda p, i: (0, 0)),
    ]
    return rows, whole, labels


def attend(qkv, column, row):
    length = qkv.shape[0]
    width = qkv.shape[1] // 3
    pairs, block = width // 128, 256
    rows, whole, labels = attention_specs(length, pairs, block)
    return pl.pallas_call(
        attend_kernel,
        grid=(pairs, length // block),
        in_specs=[rows, whole(1), whole(2)] + labels,
        out_specs=rows,
        out_shape=jax.ShapeDtypeStruct((length, width), BF16),
        compiler_params=pltpu.CompilerParams(vmem_limit_bytes=40 << 20),
        cost_estimate=pl.CostEstimate(
            flops=60 * length * length * width, bytes_accessed=8 * length * width, transcendentals=0
        ),
    )(qkv, qkv, qkv, column, row)


def attend_back(qkv, grads, column, row):
    length = qkv.shape[0]
    width = qkv.shape[1] // 3
    pairs, block = width // 128, 256
    rows, whole, labels = attention_specs(length, pairs, block)
    out = jax.ShapeDtypeStruct((length, width), BF16)
    return pl.pallas_call(
        attend_back_kernel,
        grid=(pairs, length // block),
        in_specs=[rows, whole(1), whole(2), rows] + labels,
        out_specs=[rows, whole(0), whole(0)],
        out_shape=[out, out, out],
        scratch_shapes=[pltpu.VMEM((length, 128), F32), pltpu.VMEM((length, 128), F32)],
        compiler_params=pltpu.CompilerParams(vmem_limit_bytes=48 << 20),
        cost_estimate=pl.CostEstimate(
            flops=130 * length * length * width,
            bytes_accessed=14 * length * width,
            transcendentals=0,
        ),
    )(qkv, qkv, qkv, grads, column, row)


def swap(stacked):
    count = stacked.shape[0]
    if count != 2:
        return lax.all_to_all(stacked, "ctx", 0, 0)
    place = lax.axis_index("ctx")
    mine = lax.dynamic_index_in_dim(stacked, place, 0, keepdims=False)
    sent = lax.dynamic_index_in_dim(stacked, 1 - place, 0, keepdims=False)
    got = lax.ppermute(sent, "ctx", [(0, 1), (1, 0)])
    first = place == 0
    return jnp.stack([jnp.where(first, mine, got), jnp.where(first, got, mine)])


def gather_ctx(array, count):
    if count != 2:
        return lax.all_gather(array, "ctx", axis=0, tiled=True)
    got = lax.ppermute(array, "ctx", [(0, 1), (1, 0)])
    first = lax.axis_index("ctx") == 0
    return jnp.concatenate([jnp.where(first, array, got), jnp.where(first, got, array)], axis=0)


def split_sum(value):
    high = value.astype(BF16)
    return high, (value - high.astype(F32)).astype(BF16)


def per_device(
    tokens,
    segments,
    cotangent,
    w_query,
    b_query,
    w_key,
    w_value,
    b_value,
    w_output,
    b_output,
    gain_attn,
    shift_attn,
    w_inner,
    b_inner,
    w_outer,
    b_outer,
    gain_ffn,
    shift_ffn,
):
    rows, width = tokens.shape
    seq_count = lax.axis_size("seq")
    ctx_count = lax.axis_size("ctx")
    count = seq_count * ctx_count
    place = lax.axis_index("ctx")
    part = width // ctx_count
    own = w_query.shape[0]
    wide = b_inner.shape[0]
    labels = segments[0]
    column, row = labels[:, None], labels[None, :]

    vectors = jnp.concatenate(
        [b_query, b_value, b_output, gain_attn, shift_attn, b_outer, gain_ffn, shift_ffn, b_inner]
    )
    extra = jnp.pad(vectors[None, :], ((0, 15), (0, width - vectors.shape[0])))
    packed = jnp.concatenate([w_query, w_key, w_value, w_output, extra], axis=0)
    gathered = lax.all_gather(packed, BOTH, axis=0, tiled=False)
    tokens_all = gather_ctx(tokens, ctx_count)
    winner = lax.all_gather(w_inner, BOTH, axis=0, tiled=True)
    wouter = lax.all_gather(w_outer, BOTH, axis=0, tiled=True)

    wquery, wkey, wvalue, woutput = (
        gathered[:, i * own : (i + 1) * own].reshape(width, width) for i in range(4)
    )
    small = gathered[:, 4 * own].astype(F32)
    bquery, bvalue, boutput, gattn, sattn, bouter, gffn, sffn = (
        small[:, i * own : (i + 1) * own].reshape(width) for i in range(8)
    )
    binner = small[:, 8 * own : 8 * own + wide].reshape(-1)

    def my_cols(array):
        return lax.dynamic_slice_in_dim(array, place * part, part, array.ndim - 1)

    w_three = jnp.concatenate([my_cols(wquery), my_cols(wkey), my_cols(wvalue)], axis=1)
    b_three = jnp.concatenate([my_cols(bquery), jnp.zeros((part,), F32), my_cols(bvalue)])
    qkv = (jnp.dot(tokens_all, w_three, preferred_element_type=F32) + b_three).astype(BF16)
    mixed = attend(qkv, column, row)
    mixed = swap(mixed.reshape(ctx_count, rows, part))
    attended = jnp.transpose(mixed, (1, 0, 2)).reshape(rows, width)

    pre_one = (
        tokens.astype(F32) + jnp.dot(attended, woutput, preferred_element_type=F32) + boutput
    )
    normed_one = layer_norm(pre_one, gattn, sattn)
    normed_low = normed_one.astype(BF16)
    inner = jnp.dot(normed_low, winner, preferred_element_type=F32) + binner
    act_low = exact_gelu(inner).astype(BF16)
    pre_two = normed_one + jnp.dot(act_low, wouter, preferred_element_type=F32) + bouter
    out_value = layer_norm(pre_two, gffn, sffn)

    grad_out = cotangent.astype(F32)
    _, norm_two_back = jax.vjp(layer_norm, pre_two, gffn, sffn)
    d_pre_two, d_gain_two, d_shift_two = norm_two_back(grad_out)
    outer_low = d_pre_two.astype(BF16)
    grad_bouter = jnp.sum(outer_low.astype(F32), axis=0)
    part_wouter = matmul_tn(act_low, outer_low).astype(BF16)
    out_wouter = lax.psum_scatter(part_wouter, BOTH, scatter_dimension=0, tiled=True)
    d_act = matmul_nt(outer_low, wouter)
    _, gelu_back = jax.vjp(exact_gelu, inner)
    inner_low = gelu_back(d_act)[0].astype(BF16)
    grad_binner = jnp.sum(inner_low.astype(F32), axis=0)
    part_winner = matmul_tn(normed_low, inner_low).astype(BF16)
    out_winner = lax.psum_scatter(part_winner, BOTH, scatter_dimension=0, tiled=True)
    d_normed = d_pre_two + matmul_nt(inner_low, winner)

    _, norm_one_back = jax.vjp(layer_norm, pre_one, gattn, sattn)
    d_pre_one, d_gain_one, d_shift_one = norm_one_back(d_normed)
    out_low = d_pre_one.astype(BF16)
    grad_boutput = jnp.sum(out_low.astype(F32), axis=0)
    d_attended = matmul_nt(out_low, woutput).astype(BF16)
    d_mixed = swap(jnp.transpose(d_attended.reshape(rows, ctx_count, part), (1, 0, 2)))
    d_mixed = d_mixed.reshape(ctx_count * rows, part)

    part_woutput = matmul_tn(attended, out_low).astype(BF16)
    sums = jnp.concatenate(
        [
            v.reshape(count, -1)
            for v in (
                grad_boutput, d_gain_one, d_shift_one, grad_bouter, d_gain_two, d_shift_two,
                grad_binner,
            )
        ],
        axis=1,
    )
    high, low = split_sum(sums)
    used = sums.shape[1]
    tail = jnp.pad(
        jnp.concatenate([high, low], axis=1)[:, None, :], ((0, 0), (0, 15), (0, width - 2 * used))
    )
    block = jnp.concatenate([part_woutput.reshape(count, own, width), tail], axis=1)
    block = lax.psum_scatter(block, BOTH, scatter_dimension=0, tiled=False)
    out_woutput = block[:own].astype(F32)
    sums = (block[own, :used].astype(F32) + block[own, used : 2 * used].astype(F32))
    out_boutput, out_gattn, out_sattn, out_bouter, out_gffn, out_sffn = (
        sums[i * own : (i + 1) * own] for i in range(6)
    )
    out_binner = sums[6 * own :]

    d_query, d_key, d_value = attend_back(qkv, d_mixed, column, row)
    d_three = jnp.concatenate([d_query, d_key, d_value], axis=1)

    part_three = matmul_tn(tokens_all, d_three).astype(BF16)
    bias = jnp.sum(d_three.astype(F32), axis=0)

    def spread(vector):
        whole = jnp.zeros((width,), F32)
        whole = lax.dynamic_update_slice_in_dim(whole, vector, place * part, 0)
        return whole.reshape(seq_count, ctx_count, own)

    pair = jnp.concatenate([spread(bias[:part]), spread(bias[2 * part :])], axis=2)
    high, low = split_sum(pair)
    tail = jnp.pad(
        jnp.concatenate([high, low], axis=2)[:, :, None, :],
        ((0, 0), (0, 0), (0, 15), (0, 3 * part - 4 * own)),
    )
    block = jnp.concatenate(
        [part_three.reshape(seq_count, ctx_count, own, 3 * part), tail], axis=2
    )
    block = lax.psum_scatter(block, "seq", scatter_dimension=0, tiled=False)

    d_part = matmul_nt(d_three, w_three)
    got = swap(d_part.astype(BF16).reshape(ctx_count, rows, width))
    grad_tokens = d_pre_one + jnp.sum(got.astype(F32), axis=0)

    block = swap(block).astype(F32)
    out_wquery, out_wkey, out_wvalue = (
        jnp.transpose(block[:, :own, i * part : (i + 1) * part], (1, 0, 2)).reshape(own, width)
        for i in range(3)
    )
    pair = jnp.sum(block[:, own], axis=0)
    pair = pair[: 2 * own] + pair[2 * own : 4 * own]
    out_bquery, out_bvalue = pair[:own], pair[own:]
    return (
        out_value.astype(BF16),
        grad_tokens,
        out_wquery,
        out_bquery,
        out_wkey,
        out_wvalue,
        out_bvalue,
        out_woutput,
        out_boutput,
        out_gattn,
        out_sattn,
        out_winner.astype(F32),
        out_binner,
        out_wouter.astype(F32),
        out_bouter,
        out_gffn,
        out_sffn,
    )


def solution(mesh):
    matrix, vector = P(BOTH, None), P(BOTH)
    return jax.shard_map(
        per_device,
        mesh=mesh,
        in_specs=(
            matrix, P("seq", None), matrix, matrix, vector, matrix, matrix, vector, matrix,
            vector, vector, vector, matrix, vector, matrix, vector, vector, vector,
        ),
        out_specs=(
            matrix, matrix, matrix, vector, matrix, matrix, vector, matrix, vector, vector,
            vector, matrix, vector, matrix, vector, vector, vector,
        ),
        check_vma=False,
    )
```

time: 1760 us -> 881 us (0.50)
  waiting for transfers between devices: 1150 us -> 621 us
  matrix products: 305 us -> 99.4 us
  blocking collectives: 149 us -> 0 us
  Pallas kernels: 0 us -> 66.2 us
  local copies, waits for them, and re-layouts: 91.6 us -> 40.9 us
  loops' own time: 22 us -> 0 us
    all_gather x18 -> x3, waiting for transfers between devices: 627 us -> 132 us  [the longest x1 55.4 us: per_device(): gathered = lax.all_gather(packed, BOTH, axis=0, tiled=False)]
    reduce_scatter x8 -> x4, waiting for transfers between devices: 511 us -> 420 us  [the longest x1 184 us: per_device(): lax.psum_scatter(part_wouter, BOTH, scatter_dimension=0, tiled=True)]
    dot_general x54 -> x4, matrix products: 117 us -> 29.5 us  [matmul_nt(): lax.dot_general(left, right, (((1,), (1,)), ((), ())), preferred_element_...]
    unnamed x2 -> x0, blocking collectives: 83.1 us -> none
    ppermute x0 -> x5, waiting for transfers between devices: none -> 68.5 us  [the longest x4 43.9 us: swap(): got = lax.ppermute(sent, 'ctx', [(0, 1), (1, 0)])]
    pallas_call x0 -> x2, Pallas kernels: none -> 66.2 us  [the longest x1 43 us: attend_back(): pl.pallas_call(attend_back_kernel, grid=(pairs, length // block), in_spec...]
    all_gather x1 -> x0, blocking collectives: 66.1 us -> none  [per_device(): lax.all_gather(ffn_local[1], ('seq', 'ctx'), axis=0, tiled=True)]
    dot_general x38 -> x4, matrix products: 87.6 us -> 26.5 us  [matmul_tn(): lax.dot_general(left, right, (((0,), (0,)), ((), ())), preferred_element_...]
  transfers between devices with their start and end apart: 26 -> 12, of which waited for: 22 -> 11; matrix products, arithmetic and copies ran while one was open for 13% -> 11% of each run, Pallas kernels for 0% -> 8%
where the time goes in v1:
time: 881 us; the launch traced here: 874 us
  waiting for transfers between devices  621 us (70%)
  matrix products  99.4 us (11%)
  Pallas kernels  66.2 us (8%)
  local copies, waits for them, and re-layouts  40.9 us (5%)
  other arithmetic  22.6 us (3%)
  between operations  14.9 us (2%)
  starting transfers between devices  9.39 us (1%)
    reduce_scatter x1, waiting for transfers between devices, per_device(): lax.psum_scatter(part_wouter, BOTH, scatter_dimension=0, tiled=True)  184 us
    reduce_scatter x1, waiting for transfers between devices, per_device(): lax.psum_scatter(part_winner, BOTH, scatter_dimension=0, tiled=True)  175 us
    reduce_scatter x1, waiting for transfers between devices, per_device(): block = lax.psum_scatter(block, 'seq', scatter_dimension=0, tiled=False)  61.1 us
    all_gather x1, waiting for transfers between devices, per_device(): gathered = lax.all_gather(packed, BOTH, axis=0, tiled=False)  55.4 us
    all_gather x1, waiting for transfers between devices, per_device(): wouter = lax.all_gather(w_outer, BOTH, axis=0, tiled=True)  51.2 us
    ppermute x4, waiting for transfers between devices, swap(): got = lax.ppermute(sent, 'ctx', [(0, 1), (1, 0)])  43.9 us
    pallas_call x1, Pallas kernels, attend_back(): pl.pallas_call(attend_back_kernel, grid=(pairs, length // block), in_spec...  43 us
    dot_general x4, matrix products, matmul_nt(): lax.dot_general(left, right, (((1,), (1,)), ((), ())), preferred_element_...  29.5 us
  transfers between devices with their start and end apart: 12, of which 11 were waited for; matrix products, arithmetic and copies ran while one was open for 11% of the time, Pallas kernels for 8%

profile of v1, /device:TPU:0, one launch (start us, length us, event | category | flops | bytes accessed | tf_op | source)
XLA Modules:
  0.0 874.4 jit_solution(16647989999503541106)
XLA Ops:
  7.2 0.8 constant_dynamic-update-slice_fusion.3
  8.1 6.1 concatenate.37
  14.2 0.8 constant_dynamic-update-slice_fusion.2
  15.0 0.8 constant_dynamic-update-slice_fusion.1
  15.9 0.8 constant_dynamic-update-slice_fusion
  16.7 0.7 copy-done.19
  17.5 0.7 all-gather.5.cloned.1.call-update
  18.3 3.0 collective-permute-start
  21.4 0.9 copy.48.col_ref
  22.3 24.6 %collective-permute-done = bf16[512,1024]{1,0:T(8,128)(2,1)} collective-permute-done((bf16[512,1024]{1,0:T(8,128)(2,1)}, bf16[512,1024]{1,0:T(8,128)(2,1)}, u32[]{:S(2)}, u32[]{:S(2)}) %collective-permute-start) | collective-permute-done | bytes 1048608 | tf_op jit(solution)/shard_map/ppermute | solution.py:159
  46.9 1.7 broadcast_select_fusion.1
  48.6 55.4 %all-gather.9.cloned.1.call-done = bf16[4608,1024]{1,0:T(8,128)(2,1)} async-done(((bf16[144,1024]{1,0:T(8,128)(2,1)}), bf16[4608,1024]{1,0:T(8,128)(2,1)}) %all-gather.9.cloned.1.call-update) | async-done | bytes 9437200 | tf_op jit(solution)/shard_map/all_gather | solution.py:205
  103.9 1.1 slice_convert_fusion
  105.5 5.2 fusion.37
  112.5 3.4 add_convert_fusion.1.q_ref.k_ref.v_ref
  115.9 23.2 %shard_map.305 = bf16[1024,512]{1,0:T(8,128)(2,1)S(1)} custom-call(bf16[1024,1536]{1,0:T(8,128)(2,1)S(1)} %add_convert_fusion.1.q_ref.k_ref.v_ref, bf16[1024,1536]{1,0:T(8,128)(2,1)S(1)} %add_convert_fusion.1.q_ref.k_ref.v_ref, bf16[1024,1536]{1,0:T(8,128)(2,1)S(1)} %add_convert_fusion.1.q_ref.k_ref.v_ref, s32[1024,1]{1,0:T(8,128)S(1)} %copy.48.col_ref, ...), custom_call_target="tpu_custom_call" | custom-call | flops 32212254720 | bytes 4194304 | tf_op jit(solution)/shard_map/pallas_call | solution.py:109
  139.5 1.6 collective-permute-start.1
  141.7 11.9 %collective-permute-done.1 = bf16[512,512]{0,1:T(8,128)(2,1)S(1)} collective-permute-done((bf16[512,512]{0,1:T(8,128)(2,1)S(1)}, bf16[512,512]{0,1:T(8,128)(2,1)S(1)}, u32[]{:S(2)}, u32[]{:S(2)}) %collective-permute-start.1) | collective-permute-done | bytes 524320 | tf_op jit(solution)/shard_map/ppermute | solution.py:151
  153.8 3.6 fusion.40
  157.9 25.3 %all-gather.5.cloned.1.call-done = bf16[1024,4096]{1,0:T(8,128)(2,1)} async-done(((bf16[32,4096]{1,0:T(8,128)(2,1)}), bf16[1024,4096]{1,0:T(8,128)(2,1)}) %all-gather.5.cloned.1.call-update) | async-done | bytes 8388624 | tf_op jit(solution)/shard_map/all_gather | solution.py:207
  183.1 27.8 %multiply_convert_fusion = (bf16[512,4096]{1,0:T(8,128)(2,1)}, f32[512,4096]{1,0:T(8,128)}, f32[512,4096]{1,0:T(8,128)}) fusion(f32[4096]{0:T(1024)S(1)} %slice_bitcast_fusion.1, bf16[1024,4096]{1,0:T(8,128)(2,1)} %all-gather.5.cloned.1.call-done, f32[512,1024]{1,0:T(8,128)S(1)} %get-tuple-element.82, f32[1024]{0:T(1024)S(1)} %add.148, f32[1024]{0:T(1024)S(1)} %mul.165, ...), kind=kOutput, calls=%fused_computation.6 | convolution fusion | flops 4436000768 | bytes 31485952 | tf_op jit(solution)/shard_map/dot_general | solution.py:234
  210.9 51.2 %all-gather.7.cloned.1.call-done = bf16[4096,1024]{1,0:T(8,128)(2,1)} async-done(((bf16[128,1024]{1,0:T(8,128)(2,1)}), bf16[4096,1024]{1,0:T(8,128)(2,1)}) %all-gather.7.cloned.1.call-update) | async-done | bytes 8388624 | tf_op jit(solution)/shard_map/all_gather | solution.py:208
  262.2 8.5 fusion.41
  271.1 0.8 fusion.13
  271.9 1.9 fusion.35
  274.0 13.7 %convert_reduce_fusion = (f32[4096]{0:T(1024)S(1)}, bf16[512,4096]{1,0:T(8,128)(2,1)S(1)}) fusion(f32[512,4096]{1,0:T(8,128)} %get-tuple-element.42, f32[512,4096]{1,0:T(8,128)} %get-tuple-element.83, f32[4096]{0:T(1024)S(1)} %slice_bitcast_fusion.1, bf16[512,1024]{1,0:T(8,128)(2,1)S(1)} %get-tuple-element.34, ...), kind=kOutput, calls=%fused_computation.4 | convolution fusion | flops 4330614784 | bytes 30441472 | tf_op jit(solution)/shard_map/dot_general | solution.py:33
  287.8 9.2 %multiply_reduce_fusion = (f32[1024]{0:T(1024)S(1)}, f32[512]{0:T(512)S(1)}, f32[1024]{0:T(1024)S(1)}, f32[512,1024]{1,0:T(8,128)S(1)}) fusion(f32[512,1024]{1,0:T(8,128)S(1)} %get-tuple-element.82, f32[512]{0:T(512)S(1)} %fusion.24, f32[512]{0:T(512)S(1)} %broadcast_multiply_fusion.1, f32[1024]{0:T(1024)S(1)} %mul.165, ...), kind=kOutput, calls=%fused_computation.42 | convolution fusion | flops 4300207616 | bytes 18894848 | tf_op jit(solution)/shard_map/dot_general | solution.py:33
  297.0 0.7 fusion.34
  297.8 1.3 copy-done.4
  299.3 1.0 copy-done.18
  300.3 1.3 convolution_convert_fusion.5
  301.7 0.8 reshape.212
  302.5 3.1 constant_dynamic-slice_fusion.1
  305.6 2.3 copy.70
  307.9 1.5 collective-permute-start.2
  309.4 1.7 copy.69
  311.9 2.8 convolution_convert_fusion.3
  314.7 2.1 fusion.9
  316.8 5.3 collective-permute-done.2
  322.8 43.0 %shard_map.306 = (bf16[1024,512]{1,0:T(8,128)(2,1)S(1)}, bf16[1024,512]{1,0:T(8,128)(2,1)S(1)}, bf16[1024,512]{1,0:T(8,128)(2,1)S(1)}) custom-call(bf16[1024,1536]{1,0:T(8,128)(2,1)} %copy-done.1, bf16[1024,1536]{1,0:T(8,128)(2,1)} %copy-done.1, bf16[1024,1536]{1,0:T(8,128)(2,1)} %copy-done.1, bf16[1024,512]{1,0:T(8,128)(2,1)S(1)} %bitcast.127, ...), custom_call_target="tpu_custom_call" | custom-call | flops 69793218560 | bytes 7340032 | tf_op jit(solution)/shard_map/pallas_call | solution.py:128
  367.2 5.4 convolution_convert_fusion.2
  372.6 2.7 fusion.8
  375.4 1.6 copy-done.3
  376.9 9.2 %convolution_convert_fusion.1 = bf16[1024,4096]{1,0:T(8,128)(2,1)} fusion(bf16[512,4096]{1,0:T(8,128)(2,1)} %copy-done.20, f32[512,1024]{1,0:T(8,128)S(1)} %copy-done.3, f32[1024]{0:T(1024)S(1)} %add.148, f32[1024]{0:T(1024)S(1)} %mul.165, f32[512]{0:T(512)S(1)} %fusion.24, f32[512]{0:T(512)S(1)} %broadcast_multiply_fusion.1), kind=kOutput, calls=%fused_computation.21 | convolution fusion | flops 4301783040 | bytes 14692352 | tf_op jit(solution)/shard_map/dot_general | solution.py:27
  386.2 1.1 copy-done.17
  387.4 9.1 %convolution_convert_fusion = bf16[4096,1024]{1,0:T(8,128)(2,1)} fusion(bf16[512,4096]{1,0:T(8,128)(2,1)} %get-tuple-element.41, bf16[512,1024]{1,0:T(8,128)(2,1)S(1)} %copy-done.17), kind=kOutput, calls=%fused_computation.20 | convolution fusion | flops 4299161600 | bytes 13631488 | tf_op jit(solution)/shard_map/dot_general | solution.py:27
  396.5 1.9 copy-done.8
  398.4 5.3 convolution_convert_fusion.4
  403.8 1.5 collective-permute-start.3
  405.4 23.6 %collective-permute-done.3 = bf16[512,1024]{1,0:T(8,128)(2,1)S(1)} collective-permute-done((bf16[512,1024]{1,0:T(8,128)(2,1)S(1)}, bf16[512,1024]{1,0:T(8,128)(2,1)S(1)}, u32[]{:S(2)}, u32[]{:S(2)}) %collective-permute-start.3) | collective-permute-done | bytes 1048608 | tf_op jit(solution)/shard_map/ppermute | solution.py:151
  429.6 1.6 add_add_fusion.4
  431.2 0.8 fusion.26
  432.6 1.5 fusion.23
  434.2 61.1 %reduce-scatter.5.cloned.1.call-done = bf16[1,2,48,1536]{3,2,1,0:T(8,128)(2,1)} async-done(((bf16[16,2,48,1536]{3,2,1,0:T(8,128)(2,1)}), bf16[1,2,48,1536]{3,2,1,0:T(8,128)(2,1)}) %reduce-scatter.5.cloned.1.call-update) | async-done | bytes 294928 | tf_op jit(solution)/shard_map/reduce_scatter | solution.py:307
  495.2 0.9 dynamic-slice_bitcast_fusion.1
  496.1 1.5 collective-permute-start.4
  498.2 3.1 collective-permute-done.4
  501.4 1.0 fusion.21
  502.3 0.7 copy.71
  503.7 0.7 copy.73
  505.0 174.6 %reduce-scatter.9.cloned.1.call-done = bf16[32,4096]{1,0:T(8,128)(2,1)} async-done(((bf16[1024,4096]{1,0:T(8,128)(2,1)}), bf16[32,4096]{1,0:T(8,128)(2,1)}) %reduce-scatter.9.cloned.1.call-update) | async-done | bytes 262160 | tf_op jit(solution)/shard_map/reduce_scatter | solution.py:251
  679.6 1.8 convert_element_type.145
  681.4 184.1 %reduce-scatter.11.cloned.1.call-done = bf16[128,1024]{1,0:T(8,128)(2,1)} async-done(((bf16[4096,1024]{1,0:T(8,128)(2,1)}), bf16[128,1024]{1,0:T(8,128)(2,1)}) %reduce-scatter.11.cloned.1.call-update) | async-done | bytes 262160 | tf_op jit(solution)/shard_map/reduce_scatter | solution.py:245
  865.5 1.8 convert_element_type.147
  (124 shorter events, 10.9 us)
Async XLA Ops:
  7.2 96.8 %all-gather.9.cloned.1.call-start = ((), (), s32[]{:S(2)}) async-start(), calls=%async_computation.10 | async-start | bytes 9732096 | tf_op jit(solution)/shard_map/all_gather | solution.py:205
  16.7 0.7 copy-start.19
  17.5 165.7 %all-gather.5.cloned.1.call-start = ((), (), s32[]{:S(2)}) async-start(), calls=%async_computation.4 | async-start | bytes 8650752 | tf_op jit(solution)/shard_map/all_gather | solution.py:207
  18.2 243.9 %all-gather.7.cloned.1.call-start = ((), (), s32[]{:S(2)}) async-start(), calls=%async_computation.5 | async-start | bytes 8650752 | tf_op jit(solution)/shard_map/all_gather | solution.py:208
  18.3 28.6 %collective-permute-start = (bf16[512,1024]{1,0:T(8,128)(2,1)}, bf16[512,1024]{1,0:T(8,128)(2,1)}, u32[]{:S(2)}, u32[]{:S(2)}) collective-permute-start(bf16[512,1024]{1,0:T(8,128)(2,1)} %param.18), channel_id=1, source_target_pairs={{0,1},{1,0},{2,3},{3,2},{4,5},{5,4},{6,7},{7,6},{8,9},{9,8},{10,11... | collective-permute-start | bytes 3145736 | tf_op jit(solution)/shard_map/ppermute | solution.py:159
  21.3 409.9 %reduce-scatter.7.cloned.1.call-start = ((), (), s32[]{:S(2)}) async-start(), calls=%async_computation.7 | async-start | bytes 3244032 | tf_op jit(solution)/shard_map/reduce_scatter | solution.py:279
  48.6 62.5 %copy-start.13 = (bf16[512,1024]{1,0:T(8,128)(2,1)}, bf16[512,1024]{1,0:T(8,128)(2,1)S(1)}, u32[]{:S(2)}) copy-start(bf16[512,1024]{1,0:T(8,128)(2,1)S(1)} %get-tuple-element.50) | copy-start | bytes 3145732
  48.6 62.5 %copy-start.14 = (bf16[512,1024]{1,0:T(8,128)(2,1)}, bf16[512,1024]{1,0:T(8,128)(2,1)S(1)}, u32[]{:S(2)}) copy-start(bf16[512,1024]{1,0:T(8,128)(2,1)S(1)} %get-tuple-element.51) | copy-start | bytes 3145732
  110.8 1.0 copy-start.15
  111.1 1.1 copy-start.11
  111.1 1.4 copy-start.12
  112.5 3.4 copy-start
  115.9 23.2 %copy-start.1 = (bf16[1024,1536]{1,0:T(8,128)(2,1)}, bf16[1024,1536]{1,0:T(8,128)(2,1)S(1)}, u32[]{:S(2)}) copy-start(bf16[1024,1536]{1,0:T(8,128)(2,1)S(1)} %add_convert_fusion.1.q_ref.k_ref.v_ref) | copy-start | bytes 9437188
  139.5 14.1 %collective-permute-start.1 = (bf16[512,512]{0,1:T(8,128)(2,1)S(1)}, bf16[512,512]{0,1:T(8,128)(2,1)S(1)}, u32[]{:S(2)}, u32[]{:S(2)}) collective-permute-start(bf16[512,512]{0,1:T(8,128)(2,1)S(1)} %bitcast.146), channel_id=1, source_target_pairs={{0,1},{1,0},{2,3},{3,2},{4,5},{5,4},{6,7},{7,6},{8,9},{9,8},{10,11... | collective-permute-start | bytes 1572872 | tf_op jit(solution)/shard_map/ppermute | solution.py:151
  153.8 4.0 copy-start.9
  157.5 139.5 %copy-start.2 = (f32[512,1024]{1,0:T(8,128)}, f32[512,1024]{1,0:T(8,128)S(1)}, u32[]{:S(2)}) copy-start(f32[512,1024]{1,0:T(8,128)S(1)} %get-tuple-element.82) | copy-start | bytes 6291460
  262.2 8.9 %copy-start.10 = (bf16[512,1024]{1,0:T(8,128)(2,1)S(1)}, bf16[512,1024]{1,0:T(8,128)(2,1)}, u32[]{:S(2)}) copy-start(bf16[512,1024]{1,0:T(8,128)(2,1)} %param.20) | copy-start | bytes 3145732
  274.0 13.8 %copy-start.16 = (bf16[512,1024]{1,0:T(8,128)(2,1)}, bf16[512,1024]{1,0:T(8,128)(2,1)S(1)}, u32[]{:S(2)}) copy-start(bf16[512,1024]{1,0:T(8,128)(2,1)S(1)} %get-tuple-element.34) | copy-start | bytes 3145732
  287.8 9.2 %copy-start.20 = (bf16[512,4096]{1,0:T(8,128)(2,1)}, bf16[512,4096]{1,0:T(8,128)(2,1)S(1)}, u32[]{:S(2)}) copy-start(bf16[512,4096]{1,0:T(8,128)(2,1)S(1)} %get-tuple-element.32) | copy-start | bytes 12582916
  297.0 3.3 copy-start.6
  297.7 1.3 copy-start.4
  299.3 1.0 copy-start.18
  307.9 14.1 %collective-permute-start.2 = (bf16[512,512]{0,1:T(8,128)(2,1)S(1)}, bf16[512,512]{0,1:T(8,128)(2,1)S(1)}, u32[]{:S(2)}, u32[]{:S(2)}) collective-permute-start(bf16[512,512]{0,1:T(8,128)(2,1)S(1)} %bitcast.145), channel_id=1, source_target_pairs={{0,1},{1,0},{2,3},{3,2},{4,5},{5,4},{6,7},{7,6},{8,9},{9,8},{10,11... | collective-permute-start | bytes 1572872 | tf_op jit(solution)/shard_map/ppermute | solution.py:151
  316.7 178.5 %reduce-scatter.5.cloned.1.call-start = ((), (), s32[]{:S(2)}) async-start(), calls=%async_computation.6 | async-start | bytes 5013504 | tf_op jit(solution)/shard_map/reduce_scatter | solution.py:307
  366.0 6.6 copy-start.7
  375.3 1.6 copy-start.3
  375.3 304.3 %reduce-scatter.9.cloned.1.call-start = ((), (), s32[]{:S(2)}) async-start(), calls=%async_computation.8 | async-start | bytes 8650752 | tf_op jit(solution)/shard_map/reduce_scatter | solution.py:251
  386.1 1.2 copy-start.17
  386.2 479.4 %reduce-scatter.11.cloned.1.call-start = ((), (), s32[]{:S(2)}) async-start(), calls=%async_computation.9 | async-start | bytes 8650752 | tf_op jit(solution)/shard_map/reduce_scatter | solution.py:245
  396.5 1.9 copy-start.8
  403.8 25.8 %copy-start.5 = (f32[512,1024]{1,0:T(8,128)S(1)}, f32[512,1024]{1,0:T(8,128)}, u32[]{:S(2)}) copy-start(f32[512,1024]{1,0:T(8,128)} %copy-done.4) | copy-start | bytes 6291460
  403.8 25.1 %collective-permute-start.3 = (bf16[512,1024]{1,0:T(8,128)(2,1)S(1)}, bf16[512,1024]{1,0:T(8,128)(2,1)S(1)}, u32[]{:S(2)}, u32[]{:S(2)}) collective-permute-start(bf16[512,1024]{1,0:T(8,128)(2,1)S(1)} %dynamic-slice_bitcast_fusion), channel_id=1, source_target_pairs={{0,1},{1,0},{2,3},{3,2},{4,5},{5,4},{6,7},{7,6},{8,9},{9,8},{10,11... | collective-permute-start | bytes 3145736 | tf_op jit(solution)/shard_map/ppermute | solution.py:151
  496.1 5.2 collective-permute-start.4
Sparse Core Ops, SparseCore 0:
  17.6 86.3 all-gather.8
  107.0 76.0 all-gather.4
  186.2 75.8 all-gather.6
  316.9 99.9 reduce-scatter.6
  420.6 74.6 reduce-scatter.4
  497.5 182.1 reduce-scatter.8
  682.0 183.4 reduce-scatter.10

commit v2 on v1

--- a/solution.py
+++ b/solution.py
@@ -1,5 +1,3 @@
-import functools
-
 import jax
 import jax.numpy as jnp
 from jax import lax
@@ -119,23 +117,28 @@
     )(qkv, qkv, qkv, column, row)
 
 
-def attend_back(qkv, grads, column, row):
+def attend_back(qkv, grads, column, row, pair):
     length = qkv.shape[0]
-    width = qkv.shape[1] // 3
-    pairs, block = width // 128, 256
-    rows, whole, labels = attention_specs(length, pairs, block)
-    out = jax.ShapeDtypeStruct((length, width), BF16)
+    pairs, block = qkv.shape[1] // 384, 256
+    labels = attention_specs(length, pairs, block)[2]
+    out = jax.ShapeDtypeStruct((length, 128), BF16)
+
+    def whole(third):
+        return pl.BlockSpec((length, 128), lambda p, i: (0, pair + third * pairs))
+
+    rows = pl.BlockSpec((block, 128), lambda p, i: (i, pair))
+    kept = pl.BlockSpec((length, 128), lambda p, i: (0, 0))
     return pl.pallas_call(
         attend_back_kernel,
-        grid=(pairs, length // block),
+        grid=(1, length // block),
         in_specs=[rows, whole(1), whole(2), rows] + labels,
-        out_specs=[rows, whole(0), whole(0)],
+        out_specs=[pl.BlockSpec((block, 128), lambda p, i: (i, 0)), kept, kept],
         out_shape=[out, out, out],
         scratch_shapes=[pltpu.VMEM((length, 128), F32), pltpu.VMEM((length, 128), F32)],
         compiler_params=pltpu.CompilerParams(vmem_limit_bytes=48 << 20),
         cost_estimate=pl.CostEstimate(
-            flops=130 * length * length * width,
-            bytes_accessed=14 * length * width,
+            flops=95 * length * length * 128,
+            bytes_accessed=14 * length * 128,
             transcendentals=0,
         ),
     )(qkv, qkv, qkv, grads, column, row)
@@ -159,6 +162,52 @@
     got = lax.ppermute(array, "ctx", [(0, 1), (1, 0)])
     first = lax.axis_index("ctx") == 0
     return jnp.concatenate([jnp.where(first, array, got), jnp.where(first, got, array)], axis=0)
+
+
+def halve(array, dim, place, axis, pairs):
+    mine = lax.dynamic_index_in_dim(array, place, dim, keepdims=False)
+    sent = lax.dynamic_index_in_dim(array, 1 - place, dim, keepdims=False)
+    got = lax.ppermute(sent, axis, pairs)
+    return (mine.astype(F32) + got.astype(F32)).astype(BF16)
+
+
+def sum_blocks(array, order):
+    seq_count = array.shape[0]
+    place = lax.axis_index("seq")
+    deep = seq_count // 4
+    array = array.reshape((deep, 2, 2) + array.shape[1:])
+    left = ["z", "x", "core", "y"]
+    for name in order:
+        dim = left.index(name)
+        if name == "core":
+            pairs = [(i, i ^ 1) for i in range(seq_count)]
+            array = halve(array, dim, lax.rem(place, 2), "seq", pairs)
+        elif name == "x":
+            pairs = [(i, i ^ 2) for i in range(seq_count)]
+            array = halve(array, dim, lax.rem(place // 2, 2), "seq", pairs)
+        else:
+            array = halve(array, dim, lax.axis_index("ctx"), "ctx", [(0, 1), (1, 0)])
+        left.remove(name)
+    level = place // 4
+    total = lax.dynamic_index_in_dim(array, level, 0, keepdims=False).astype(F32)
+    for step in range(1, deep):
+        sent = lax.dynamic_index_in_dim(array, lax.rem(level + step, deep), 0, keepdims=False)
+        pairs = [(i, (i + 4 * step) % seq_count) for i in range(seq_count)]
+        total += lax.ppermute(sent, "seq", pairs).astype(F32)
+    return total
+
+
+def sum_all(array, order):
+    seq_count, ctx_count = lax.axis_size("seq"), lax.axis_size("ctx")
+    if ctx_count != 2:
+        return lax.psum_scatter(array, BOTH, scatter_dimension=0, tiled=False).astype(F32)
+    return sum_blocks(array.reshape((seq_count, ctx_count) + array.shape[1:]), order)
+
+
+def sum_seq(array):
+    if lax.axis_size("ctx") != 2:
+        return lax.psum_scatter(array, "seq", scatter_dimension=0, tiled=False)
+    return sum_blocks(array, ("core", "x")).astype(BF16)
 
 
 def split_sum(value):
@@ -242,23 +291,19 @@
     outer_low = d_pre_two.astype(BF16)
     grad_bouter = jnp.sum(outer_low.astype(F32), axis=0)
     part_wouter = matmul_tn(act_low, outer_low).astype(BF16)
-    out_wouter = lax.psum_scatter(part_wouter, BOTH, scatter_dimension=0, tiled=True)
+    part_wouter = part_wouter.reshape(count, wide, width)
     d_act = matmul_nt(outer_low, wouter)
     _, gelu_back = jax.vjp(exact_gelu, inner)
     inner_low = gelu_back(d_act)[0].astype(BF16)
     grad_binner = jnp.sum(inner_low.astype(F32), axis=0)
     part_winner = matmul_tn(normed_low, inner_low).astype(BF16)
-    out_winner = lax.psum_scatter(part_winner, BOTH, scatter_dimension=0, tiled=True)
+    part_winner = part_winner.reshape(count, own, wide * count)
     d_normed = d_pre_two + matmul_nt(inner_low, winner)
 
     _, norm_one_back = jax.vjp(layer_norm, pre_one, gattn, sattn)
     d_pre_one, d_gain_one, d_shift_one = norm_one_back(d_normed)
     out_low = d_pre_one.astype(BF16)
     grad_boutput = jnp.sum(out_low.astype(F32), axis=0)
-    d_attended = matmul_nt(out_low, woutput).astype(BF16)
-    d_mixed = swap(jnp.transpose(d_attended.reshape(rows, ctx_count, part), (1, 0, 2)))
-    d_mixed = d_mixed.reshape(ctx_count * rows, part)
-
     part_woutput = matmul_tn(attended, out_low).astype(BF16)
     sums = jnp.concatenate(
         [
@@ -276,7 +321,16 @@
         jnp.concatenate([high, low], axis=1)[:, None, :], ((0, 0), (0, 15), (0, width - 2 * used))
     )
     block = jnp.concatenate([part_woutput.reshape(count, own, width), tail], axis=1)
-    block = lax.psum_scatter(block, BOTH, scatter_dimension=0, tiled=False)
+    out_low, part_wouter, part_winner, block = lax.optimization_barrier(
+        (out_low, part_wouter, part_winner, block)
+    )
+    out_wouter = sum_all(part_wouter, ("core", "x", "y"))
+    out_winner = sum_all(part_winner, ("core", "y", "x"))
+    d_attended = matmul_nt(out_low, woutput).astype(BF16)
+    d_mixed = swap(jnp.transpose(d_attended.reshape(rows, ctx_count, part), (1, 0, 2)))
+    d_mixed = d_mixed.reshape(ctx_count * rows, part)
+
+    block = sum_all(block, ("core", "y", "x"))
     out_woutput = block[:own].astype(F32)
     sums = (block[own, :used].astype(F32) + block[own, used : 2 * used].astype(F32))
     out_boutput, out_gattn, out_sattn, out_bouter, out_gffn, out_sffn = (
@@ -284,8 +338,8 @@
     )
     out_binner = sums[6 * own :]
 
-    d_query, d_key, d_value = attend_back(qkv, d_mixed, column, row)
-    d_three = jnp.concatenate([d_query, d_key, d_value], axis=1)
+    backs = [attend_back(qkv, d_mixed, column, row, pair) for pair in range(part // 128)]
+    d_three = jnp.concatenate([back[i] for i in range(3) for back in backs], axis=1)
 
     part_three = matmul_tn(tokens_all, d_three).astype(BF16)
     bias = jnp.sum(d_three.astype(F32), axis=0)
@@ -304,7 +358,7 @@
     block = jnp.concatenate(
         [part_three.reshape(seq_count, ctx_count, own, 3 * part), tail], axis=2
     )
-    block = lax.psum_scatter(block, "seq", scatter_dimension=0, tiled=False)
+    block = sum_seq(block)
 
     d_part = matmul_nt(d_three, w_three)
     got = swap(d_part.astype(BF16).reshape(ctx_count, rows, width))
@@ -330,9 +384,9 @@
         out_boutput,
         out_gattn,
         out_sattn,
-        out_winner.astype(F32),
+        out_winner,
         out_binner,
-        out_wouter.astype(F32),
+        out_wouter,
         out_bouter,
         out_gffn,
         out_sffn,

time: 881 us -> 618 us (0.70)
  waiting for transfers between devices: 621 us -> 303 us
  starting transfers between devices: 9.39 us -> 46.8 us
  local copies, waits for them, and re-layouts: 40.9 us -> 57 us
  other arithmetic: 22.6 us -> 34.7 us
  matrix products: 99.4 us -> 89.7 us
    reduce_scatter x4 -> x0, waiting for transfers between devices: 420 us -> none  [the longest x1 184 us: per_device(): lax.psum_scatter(part_wouter, BOTH, scatter_dimension=0, tiled=True)]
    ppermute x0 -> x23, waiting for transfers between devices: none -> 129 us  [the longest x11 86.5 us: halve(): got = lax.ppermute(sent, axis, pairs)]
    ppermute x0 -> x23, starting transfers between devices: none -> 38.3 us  [the longest x12 30.4 us: sum_blocks(): total += lax.ppermute(sent, 'seq', pairs).astype(F32)]
    ppermute x4, waiting for transfers between devices: 43.9 us -> 17.2 us  [swap(): got = lax.ppermute(sent, 'ctx', [(0, 1), (1, 0)])]
    squeeze x0 -> x14, local copies, waits for them, and re-layouts: none -> 15 us  [the longest x10 14 us: halve(): sent = lax.dynamic_index_in_dim(array, 1 - place, dim, keepdims=False)]
    convert_element_type x3 -> x12, other arithmetic: 5.1 us -> 18.2 us  [the longest x11 16.9 us: halve(): return (mine.astype(F32) + got.astype(F32)).astype(BF16)]
    pallas_call x1 -> x4, Pallas kernels: 43 us -> 41.2 us  [attend_back(): pl.pallas_call(attend_back_kernel, grid=(1, length // block), in_specs=[r...]
  transfers between devices with their start and end apart: 12 -> 31, of which waited for: 11 -> 19; matrix products, arithmetic and copies ran while one was open for 11% -> 17% of each run, Pallas kernels for 8% -> 11%
where the time goes in v2:
time: 618 us; the launch traced here: 611 us
  waiting for transfers between devices  303 us (49%)
  matrix products  89.7 us (15%)
  Pallas kernels  64.4 us (10%)
  local copies, waits for them, and re-layouts  57 us (9%)
  starting transfers between devices  46.8 us (8%)
  other arithmetic  34.7 us (6%)
  between operations  15.2 us (2%)
    ppermute x11, waiting for transfers between devices, halve(): got = lax.ppermute(sent, axis, pairs)  86.5 us
    all_gather x1, waiting for transfers between devices, per_device(): gathered = lax.all_gather(packed, BOTH, axis=0, tiled=False)  55.4 us
    all_gather x1, waiting for transfers between devices, per_device(): wouter = lax.all_gather(w_outer, BOTH, axis=0, tiled=True)  51.4 us
    ppermute x12, waiting for transfers between devices, sum_blocks(): total += lax.ppermute(sent, 'seq', pairs).astype(F32)  42 us
    pallas_call x4, Pallas kernels, attend_back(): pl.pallas_call(attend_back_kernel, grid=(1, length // block), in_specs=[r...  41.2 us
    ppermute x12, starting transfers between devices, sum_blocks(): total += lax.ppermute(sent, 'seq', pairs).astype(F32)  30.4 us
    dot_general x1, matrix products, per_device(): inner = jnp.dot(normed_low, winner, preferred_element_type=F32) + binner  27.8 us
    dot_general x4, matrix products, matmul_nt(): lax.dot_general(left, right, (((1,), (1,)), ((), ())), preferred_element_...  27.4 us
  transfers between devices with their start and end apart: 31, of which 19 were waited for; matrix products, arithmetic and copies ran while one was open for 17% of the time, Pallas kernels for 11%

profile of v2, /device:TPU:0, one launch (start us, length us, event | category | flops | bytes accessed | tf_op | source)
XLA Modules:
  0.0 610.9 jit_solution(8509694227739950516)
XLA Ops:
  8.1 6.1 concatenate.42
  18.3 3.0 collective-permute-start
  22.2 24.6 %collective-permute-done = bf16[512,1024]{1,0:T(8,128)(2,1)} collective-permute-done((bf16[512,1024]{1,0:T(8,128)(2,1)}, bf16[512,1024]{1,0:T(8,128)(2,1)}, u32[]{:S(2)}, u32[]{:S(2)}) %collective-permute-start) | collective-permute-done | bytes 1048608 | tf_op jit(solution)/shard_map/ppermute | solution.py:162
  46.9 1.7 broadcast_select_fusion.1
  48.6 55.4 %all-gather.9.cloned.1.call-done = bf16[4608,1024]{1,0:T(8,128)(2,1)} async-done(((bf16[144,1024]{1,0:T(8,128)(2,1)}), bf16[4608,1024]{1,0:T(8,128)(2,1)}) %all-gather.9.cloned.1.call-update) | async-done | bytes 9437200 | tf_op jit(solution)/shard_map/all_gather | solution.py:254
  105.5 5.2 fusion.57
  112.5 3.4 add_convert_fusion.1.q_ref.k_ref.v_ref
  115.9 23.2 %shard_map.305 = bf16[1024,512]{1,0:T(8,128)(2,1)S(1)} custom-call(bf16[1024,1536]{1,0:T(8,128)(2,1)S(1)} %add_convert_fusion.1.q_ref.k_ref.v_ref, bf16[1024,1536]{1,0:T(8,128)(2,1)S(1)} %add_convert_fusion.1.q_ref.k_ref.v_ref, bf16[1024,1536]{1,0:T(8,128)(2,1)S(1)} %add_convert_fusion.1.q_ref.k_ref.v_ref, s32[1024,1]{1,0:T(8,128)S(1)} %copy.51.col_ref, ...), custom_call_target="tpu_custom_call" | custom-call | flops 32212254720 | bytes 4194304 | tf_op jit(solution)/shard_map/pallas_call | solution.py:107
  139.5 1.5 collective-permute-start.1
  141.7 12.0 %collective-permute-done.1 = bf16[512,512]{0,1:T(8,128)(2,1)S(1)} collective-permute-done((bf16[512,512]{0,1:T(8,128)(2,1)S(1)}, bf16[512,512]{0,1:T(8,128)(2,1)S(1)}, u32[]{:S(2)}, u32[]{:S(2)}) %collective-permute-start.1) | collective-permute-done | bytes 524320 | tf_op jit(solution)/shard_map/ppermute | solution.py:154
  153.8 3.6 fusion.60
  157.8 25.3 %all-gather.5.cloned.1.call-done = bf16[1024,4096]{1,0:T(8,128)(2,1)} async-done(((bf16[32,4096]{1,0:T(8,128)(2,1)}), bf16[1024,4096]{1,0:T(8,128)(2,1)}) %all-gather.5.cloned.1.call-update) | async-done | bytes 8388624 | tf_op jit(solution)/shard_map/all_gather | solution.py:256
  183.1 27.8 %multiply_convert_fusion = (bf16[512,4096]{1,0:T(8,128)(2,1)}, f32[512,4096]{1,0:T(8,128)}, f32[512,4096]{1,0:T(8,128)}) fusion(f32[4096]{0:T(1024)S(1)} %slice_bitcast_fusion, bf16[1024,4096]{1,0:T(8,128)(2,1)} %all-gather.5.cloned.1.call-done, f32[512,1024]{1,0:T(8,128)S(1)} %get-tuple-element.120, f32[1024]{0:T(1024)S(1)} %add.300, f32[1024]{0:T(1024)S(1)} %mul.165, ...), kind=kOutput, calls=%fused_computation.8 | convolution fusion | flops 4436000768 | bytes 31485952 | tf_op jit(solution)/shard_map/dot_general | solution.py:283
  210.9 51.4 %all-gather.7.cloned.1.call-done = bf16[4096,1024]{1,0:T(8,128)(2,1)} async-done(((bf16[128,1024]{1,0:T(8,128)(2,1)}), bf16[4096,1024]{1,0:T(8,128)(2,1)}) %all-gather.7.cloned.1.call-update) | async-done | bytes 8388624 | tf_op jit(solution)/shard_map/all_gather | solution.py:257
  262.3 8.5 %fusion.61 = (f32[512]{0:T(512)S(1)}, f32[512,1024]{1,0:T(8,128)S(1)}) fusion(f32[1024]{0:T(1024)S(1)} %add.307, bf16[512,4096]{1,0:T(8,128)(2,1)} %get-tuple-element.67, bf16[4096,1024]{1,0:T(8,128)(2,1)} %all-gather.7.cloned.1.call-done, f32[1024]{0:T(1024)S(1)} %add.300, f32[1024]{0:T(1024)S(1)} %mul.165, f32[512]{0:T(512)S(1)} %fusion.45, ...), kind=kOutput, calls=%fused_computation.214 | convolution fusion | flops 4298636800 | bytes 16795648 | tf_op jit(solution)/shard_map/dot_general | solution.py:285
  272.0 1.9 fusion.55
  274.6 6.8 %convolution_convert_fusion.1 = bf16[4096,1024]{1,0:T(8,128)(2,1)} fusion(bf16[512,4096]{1,0:T(8,128)(2,1)S(1)} %copy-done.25, bf16[512,1024]{1,0:T(8,128)(2,1)S(1)} %get-tuple-element.60), kind=kOutput, calls=%fused_computation.23 | convolution fusion | flops 4299161600 | bytes 13631488 | tf_op jit(solution)/shard_map/dot_general | solution.py:25
  281.4 13.8 %convert_reduce_fusion = (f32[4096]{0:T(1024)S(1)}, bf16[512,4096]{1,0:T(8,128)(2,1)S(1)}) fusion(f32[512,4096]{1,0:T(8,128)} %get-tuple-element.68, f32[512,4096]{1,0:T(8,128)} %get-tuple-element.121, f32[4096]{0:T(1024)S(1)} %slice_bitcast_fusion, bf16[512,1024]{1,0:T(8,128)(2,1)S(1)} %get-tuple-element.60, bf16[4096,1024]{1,0:T(8,128)(2,1)} %all-gather.7.cloned.1.call-done), kind=kOutput, calls=%fused_computation.6 | convolution fusion | flops 4330614784 | bytes 30441472 | tf_op jit(solution)/shard_map/dot_general | solution.py:31
  295.2 7.2 %convolution_convert_fusion = bf16[1024,4096]{1,0:T(8,128)(2,1)} fusion(bf16[512,4096]{1,0:T(8,128)(2,1)S(1)} %get-tuple-element.58, f32[512,1024]{1,0:T(8,128)S(1)} %get-tuple-element.120, f32[1024]{0:T(1024)S(1)} %add.300, f32[1024]{0:T(1024)S(1)} %mul.165, f32[512]{0:T(512)S(1)} %fusion.45, f32[512]{0:T(512)S(1)} %broadcast_multiply_fusion.1), kind=kOutput, calls=%fused_computation.22 | convolution fusion | flops 4301783040 | bytes 14692352 | tf_op jit(solution)/shard_map/dot_general | solution.py:25
  302.4 7.7 %multiply_reduce_fusion = (f32[1024]{0:T(1024)S(1)}, f32[512]{0:T(512)S(1)}, f32[1024]{0:T(1024)S(1)}, f32[512,1024]{1,0:T(8,128)S(1)}) fusion(f32[512,1024]{1,0:T(8,128)S(1)} %get-tuple-element.120, f32[512]{0:T(512)S(1)} %fusion.45, f32[512]{0:T(512)S(1)} %broadcast_multiply_fusion.1, f32[1024]{0:T(1024)S(1)} %mul.165, ...), kind=kOutput, calls=%fused_computation.69 | convolution fusion | flops 4300207616 | bytes 18894848 | tf_op jit(solution)/shard_map/dot_general | solution.py:31
  314.4 2.0 fusion.12
  316.4 2.3 convolution_convert_fusion.5
  318.7 2.0 reshape.251
  320.7 3.1 constant_dynamic-slice_fusion.1
  323.9 2.3 copy.77
  326.2 1.6 collective-permute-start.2
  329.1 2.7 dynamic-slice_bitcast_fusion.4
  331.8 4.7 dynamic-slice_bitcast_fusion.1
  337.0 3.3 collective-permute-done.2
  341.1 1.9 copy-done.2
  343.0 10.2 %shard_map.306 = (bf16[1024,128]{1,0:T(8,128)(2,1)S(1)}, bf16[1024,128]{1,0:T(8,128)(2,1)S(1)}, bf16[1024,128]{1,0:T(8,128)(2,1)S(1)}) custom-call(bf16[1024,1536]{1,0:T(8,128)(2,1)S(1)} %copy-done.2, bf16[1024,1536]{1,0:T(8,128)(2,1)S(1)} %copy-done.2, bf16[1024,1536]{1,0:T(8,128)(2,1)S(1)} %copy-done.2, bf16[1024,512]{1,0:T(8,128)(2,1)S(1)} %bitcast.220, ...), custom_call_target="tpu_custom_call" | custom-call | flops 12750684160 | bytes 1835008 | tf_op jit(solution)/shard_map/pallas_call | solution.py:131
  353.2 10.2 %shard_map.307 = (bf16[1024,128]{1,0:T(8,128)(2,1)S(1)}, bf16[1024,128]{1,0:T(8,128)(2,1)S(1)}, bf16[1024,128]{1,0:T(8,128)(2,1)S(1)}) custom-call(bf16[1024,1536]{1,0:T(8,128)(2,1)S(1)} %copy-done.2, bf16[1024,1536]{1,0:T(8,128)(2,1)S(1)} %copy-done.2, bf16[1024,1536]{1,0:T(8,128)(2,1)S(1)} %copy-done.2, bf16[1024,512]{1,0:T(8,128)(2,1)S(1)} %bitcast.221, ...), custom_call_target="tpu_custom_call" | custom-call | flops 12750684160 | bytes 1835008 | tf_op jit(solution)/shard_map/pallas_call | solution.py:131
  363.5 10.2 %shard_map.308 = (bf16[1024,128]{1,0:T(8,128)(2,1)S(1)}, bf16[1024,128]{1,0:T(8,128)(2,1)S(1)}, bf16[1024,128]{1,0:T(8,128)(2,1)S(1)}) custom-call(bf16[1024,1536]{1,0:T(8,128)(2,1)S(1)} %copy-done.2, bf16[1024,1536]{1,0:T(8,128)(2,1)S(1)} %copy-done.2, bf16[1024,1536]{1,0:T(8,128)(2,1)S(1)} %copy-done.2, bf16[1024,512]{1,0:T(8,128)(2,1)S(1)} %bitcast.222, ...), custom_call_target="tpu_custom_call" | custom-call | flops 12750684160 | bytes 1835008 | tf_op jit(solution)/shard_map/pallas_call | solution.py:131
  373.7 10.5 %shard_map.309 = (bf16[1024,128]{1,0:T(8,128)(2,1)S(1)}, bf16[1024,128]{1,0:T(8,128)(2,1)S(1)}, bf16[1024,128]{1,0:T(8,128)(2,1)S(1)}) custom-call(bf16[1024,1536]{1,0:T(8,128)(2,1)S(1)} %copy-done.2, bf16[1024,1536]{1,0:T(8,128)(2,1)S(1)} %copy-done.2, bf16[1024,1536]{1,0:T(8,128)(2,1)S(1)} %copy-done.2, bf16[1024,512]{1,0:T(8,128)(2,1)S(1)} %bitcast.223, ...), custom_call_target="tpu_custom_call" | custom-call | flops 12750684160 | bytes 1835008 | tf_op jit(solution)/shard_map/pallas_call | solution.py:131
  386.0 3.7 convolution_convert_fusion.3
  390.8 1.5 collective-permute-start.3
  392.9 3.7 convolution_convert_fusion.2
  396.7 2.1 fusion.13
  402.9 29.6 %collective-permute-done.11 = bf16[4,2,48,1024]{3,2,1,0:T(8,128)(2,1)} collective-permute-done((bf16[4,2,48,1024]{3,2,1,0:T(8,128)(2,1)}, bf16[4,2,48,1024]{3,2,1,0:T(8,128)(2,1)}, u32[]{:S(2)}, u32[]{:S(2)}) %collective-permute-start.11) | collective-permute-done | bytes 786464 | tf_op jit(solution)/shard_map/ppermute | solution.py:170
  432.5 1.4 fusion.26
  434.0 1.5 collective-permute-start.12
  435.5 4.9 dynamic-slice_bitcast_fusion
  440.4 1.4 fusion.27
  441.8 1.8 collective-permute-done.12
  443.7 1.9 collective-permute-start.15
  448.4 5.3 collective-permute-start.13
  453.8 1.6 add_add_fusion.4
  458.8 1.3 collective-permute-start.5
  460.1 5.3 fusion.2
  466.9 16.6 %collective-permute-done.5 = bf16[4,2,48,1536]{3,2,1,0:T(8,128)(2,1)S(1)} collective-permute-done((bf16[4,2,48,1536]{3,2,1,0:T(8,128)(2,1)S(1)}, bf16[4,2,48,1536]{3,2,1,0:T(8,128)(2,1)S(1)}, u32[]{:S(2)}, u32[]{:S(2)}) %collective-permute-start.5) | collective-permute-done | bytes 1179680 | tf_op jit(solution)/shard_map/ppermute | solution.py:170
  484.8 2.0 collective-permute-start.8
  487.1 2.0 collective-permute-start.6
  489.1 4.3 fusion.1
  494.6 15.3 %collective-permute-done.7 = bf16[2,48,1536]{2,1,0:T(8,128)(2,1)} collective-permute-done((bf16[2,48,1536]{2,1,0:T(8,128)(2,1)}, bf16[2,48,1536]{2,1,0:T(8,128)(2,1)}, u32[]{:S(2)}, u32[]{:S(2)}) %collective-permute-start.7) | collective-permute-done | bytes 294944 | tf_op jit(solution)/shard_map/ppermute | solution.py:196
  512.9 1.5 collective-permute-start.18
  514.5 1.9 collective-permute-done.9
  519.1 23.1 %collective-permute-done.23 = bf16[4,2,128,1024]{3,2,1,0:T(8,128)(2,1)S(1)} collective-permute-done((bf16[4,2,128,1024]{3,2,1,0:T(8,128)(2,1)S(1)}, bf16[4,2,128,1024]{3,2,1,0:T(8,128)(2,1)S(1)}, u32[]{:S(2)}, u32[]{:S(2)}) %collective-permute-start.23) | collective-permute-done | bytes 2097184 | tf_op jit(solution)/shard_map/ppermute | solution.py:170
  543.8 15.4 %collective-permute-done.18 = bf16[4,32,4096]{2,1,0:T(8,128)(2,1)S(1)} collective-permute-done((bf16[4,32,4096]{2,1,0:T(8,128)(2,1)S(1)}, bf16[4,32,4096]{2,1,0:T(8,128)(2,1)S(1)}, u32[]{:S(2)}, u32[]{:S(2)}) %collective-permute-start.18) | collective-permute-done | bytes 1048608 | tf_op jit(solution)/shard_map/ppermute | solution.py:170
  559.5 2.2 collective-permute-start.21
  563.3 3.6 collective-permute-start.27
  567.2 3.9 collective-permute-done.21
  571.1 10.5 %collective-permute-start.25 = (bf16[128,1024]{1,0:T(8,128)(2,1)S(1)}, bf16[128,1024]{1,0:T(8,128)(2,1)S(1)}, u32[]{:S(2)}, u32[]{:S(2)}) collective-permute-start(bf16[128,1024]{1,0:T(8,128)(2,1)S(1)} %get-tuple-element.81), channel_id=1, source_target_pairs={{0,8},{2,10},{4,12},{6,14},{8,16},{10,18},{12,20},{14,22},{16,24},... | collective-permute-start | bytes 786440 | tf_op jit(solution)/shard_map/ppermute | solution.py:196
  581.6 13.2 %collective-permute-done.20 = bf16[32,4096]{1,0:T(8,128)(2,1)S(1)} collective-permute-done((bf16[32,4096]{1,0:T(8,128)(2,1)S(1)}, bf16[32,4096]{1,0:T(8,128)(2,1)S(1)}, u32[]{:S(2)}, u32[]{:S(2)}) %collective-permute-start.20) | collective-permute-done | bytes 262176 | tf_op jit(solution)/shard_map/ppermute | solution.py:196
  595.7 7.3 %collective-permute-done.26 = bf16[128,1024]{1,0:T(8,128)(2,1)S(1)} collective-permute-done((bf16[128,1024]{1,0:T(8,128)(2,1)S(1)}, bf16[128,1024]{1,0:T(8,128)(2,1)S(1)}, u32[]{:S(2)}, u32[]{:S(2)}) %collective-permute-start.26) | collective-permute-done | bytes 262176 | tf_op jit(solution)/shard_map/ppermute | solution.py:196
  (213 shorter events, 48.7 us)
Async XLA Ops:
  7.2 96.8 %all-gather.9.cloned.1.call-start = ((), (), s32[]{:S(2)}) async-start(), calls=%async_computation.2 | async-start | bytes 9732096 | tf_op jit(solution)/shard_map/all_gather | solution.py:254
  16.7 0.7 copy-start.24
  17.5 165.7 %all-gather.5.cloned.1.call-start = ((), (), s32[]{:S(2)}) async-start(), calls=%async_computation | async-start | bytes 8650752 | tf_op jit(solution)/shard_map/all_gather | solution.py:256
  18.2 244.1 %all-gather.7.cloned.1.call-start = ((), (), s32[]{:S(2)}) async-start(), calls=%async_computation.1 | async-start | bytes 8650752 | tf_op jit(solution)/shard_map/all_gather | solution.py:257
  18.3 28.6 %collective-permute-start = (bf16[512,1024]{1,0:T(8,128)(2,1)}, bf16[512,1024]{1,0:T(8,128)(2,1)}, u32[]{:S(2)}, u32[]{:S(2)}) collective-permute-start(bf16[512,1024]{1,0:T(8,128)(2,1)} %param.18), channel_id=1, source_target_pairs={{0,1},{1,0},{2,3},{3,2},{4,5},{5,4},{6,7},{7,6},{8,9},{9,8},{10,11... | collective-permute-start | bytes 3145736 | tf_op jit(solution)/shard_map/ppermute | solution.py:162
  48.6 62.5 %copy-start.14 = (bf16[512,1024]{1,0:T(8,128)(2,1)}, bf16[512,1024]{1,0:T(8,128)(2,1)S(1)}, u32[]{:S(2)}) copy-start(bf16[512,1024]{1,0:T(8,128)(2,1)S(1)} %get-tuple-element.76) | copy-start | bytes 3145732
  48.6 62.5 %copy-start.16 = (bf16[512,1024]{1,0:T(8,128)(2,1)}, bf16[512,1024]{1,0:T(8,128)(2,1)S(1)}, u32[]{:S(2)}) copy-start(bf16[512,1024]{1,0:T(8,128)(2,1)S(1)} %get-tuple-element.77) | copy-start | bytes 3145732
  110.8 1.0 copy-start.22
  111.1 1.0 copy-start.18
  111.1 1.4 copy-start.20
  112.5 3.4 copy-start
  115.9 23.2 %copy-start.1 = (bf16[1024,1536]{1,0:T(8,128)(2,1)}, bf16[1024,1536]{1,0:T(8,128)(2,1)S(1)}, u32[]{:S(2)}) copy-start(bf16[1024,1536]{1,0:T(8,128)(2,1)S(1)} %add_convert_fusion.1.q_ref.k_ref.v_ref) | copy-start | bytes 9437188
  139.5 14.2 %collective-permute-start.1 = (bf16[512,512]{0,1:T(8,128)(2,1)S(1)}, bf16[512,512]{0,1:T(8,128)(2,1)S(1)}, u32[]{:S(2)}, u32[]{:S(2)}) collective-permute-start(bf16[512,512]{0,1:T(8,128)(2,1)S(1)} %bitcast.253), channel_id=1, source_target_pairs={{0,1},{1,0},{2,3},{3,2},{4,5},{5,4},{6,7},{7,6},{8,9},{9,8},{10,11... | collective-permute-start | bytes 1572872 | tf_op jit(solution)/shard_map/ppermute | solution.py:154
  153.8 3.7 copy-start.9
  262.3 8.9 %copy-start.11 = (bf16[512,1024]{1,0:T(8,128)(2,1)S(1)}, bf16[512,1024]{1,0:T(8,128)(2,1)}, u32[]{:S(2)}) copy-start(bf16[512,1024]{1,0:T(8,128)(2,1)} %param.20) | copy-start | bytes 3145732
  272.0 2.6 copy-start.25
  310.8 1.4 copy-start.3
  310.8 2.3 copy-start.10
  314.4 2.1 copy-start.6
  326.2 14.2 %collective-permute-start.2 = (bf16[512,512]{0,1:T(8,128)(2,1)S(1)}, bf16[512,512]{0,1:T(8,128)(2,1)S(1)}, u32[]{:S(2)}, u32[]{:S(2)}) collective-permute-start(bf16[512,512]{0,1:T(8,128)(2,1)S(1)} %bitcast.252), channel_id=1, source_target_pairs={{0,1},{1,0},{2,3},{3,2},{4,5},{5,4},{6,7},{7,6},{8,9},{9,8},{10,11... | collective-permute-start | bytes 1572872 | tf_op jit(solution)/shard_map/ppermute | solution.py:154
  331.8 64.9 %collective-permute-start.10 = (bf16[4,2,2,48,1024]{4,3,2,1,0:T(8,128)(2,1)}, bf16[4,2,2,48,1024]{4,3,2,1,0:T(8,128)(2,1)}, u32[]{:S(2)}, u32[]{:S(2)}) collective-permute-start(bf16[4,2,2,48,1024]{4,3,2,1,0:T(8,128)(2,1)} %dynamic-slice_bitcast_fusion.4), channel_id=1, source_target_pairs={{0,2},{2,0},{4,6},{6,4},{8,10},{10,8},{12,14},{14,12},{16,18},{18,... | collective-permute-start | bytes 4718600 | tf_op jit(solution)/shard_map/ppermute | solution.py:170
  336.5 123.6 %collective-permute-start.16 = (bf16[4,2,2,32,4096]{4,3,2,1,0:T(8,128)(2,1)}, bf16[4,2,2,32,4096]{4,3,2,1,0:T(8,128)(2,1)}, u32[]{:S(2)}, u32[]{:S(2)}) collective-permute-start(bf16[4,2,2,32,4096]{4,3,2,1,0:T(8,128)(2,1)} %dynamic-slice_bitcast_fusion.1), channel_id=1, source_target_pairs={{0,2},{2,0},{4,6},{6,4},{8,10},{10,8},{12,14},{14,12},{16,18},{18,... | collective-permute-start | bytes 12582920 | tf_op jit(solution)/shard_map/ppermute | solution.py:170
  341.1 1.9 copy-start.2
  384.2 1.2 copy-start.19
  384.2 1.5 copy-start.21
  384.2 1.8 copy-start.23
  389.7 6.9 %copy-start.12 = (bf16[1024,1024]{1,0:T(8,128)(2,1)}, bf16[1024,1024]{1,0:T(8,128)(2,1)S(1)}, u32[]{:S(2)}) copy-start(bf16[1024,1024]{1,0:T(8,128)(2,1)S(1)} %convolution_convert_fusion.3) | copy-start | bytes 6291460
  389.7 3.2 copy-start.15
  389.7 3.2 copy-start.17
  390.8 49.5 %collective-permute-start.3 = (bf16[512,1024]{1,0:T(8,128)(2,1)}, bf16[512,1024]{1,0:T(8,128)(2,1)}, u32[]{:S(2)}, u32[]{:S(2)}) collective-permute-start(bf16[512,1024]{1,0:T(8,128)(2,1)} %dynamic-slice_bitcast_fusion.8), channel_id=1, source_target_pairs={{0,1},{1,0},{2,3},{3,2},{4,5},{5,4},{6,7},{7,6},{8,9},{9,8},{10,11... | collective-permute-start | bytes 3145736 | tf_op jit(solution)/shard_map/ppermute | solution.py:154
  392.9 3.7 copy-start.5
  398.8 1.2 copy-start.7
  400.9 31.6 %collective-permute-start.11 = (bf16[4,2,48,1024]{3,2,1,0:T(8,128)(2,1)}, bf16[4,2,48,1024]{3,2,1,0:T(8,128)(2,1)}, u32[]{:S(2)}, u32[]{:S(2)}) collective-permute-start(bf16[4,2,48,1024]{3,2,1,0:T(8,128)(2,1)} %dynamic-slice_bitcast_fusion.9), channel_id=1, source_target_pairs={{0,1},{1,0},{2,3},{3,2},{4,5},{5,4},{6,7},{7,6},{8,9},{9,8},{10,11... | collective-permute-start | bytes 2359304 | tf_op jit(solution)/shard_map/ppermute | solution.py:170
  402.6 29.9 %copy-start.8 = (bf16[4,2,2,48,1024]{4,3,2,1,0:T(8,128)(2,1)S(1)}, bf16[4,2,2,48,1024]{4,3,2,1,0:T(8,128)(2,1)}, u32[]{:S(2)}) copy-start(bf16[4,2,2,48,1024]{4,3,2,1,0:T(8,128)(2,1)} %copy-done.7) | copy-start | bytes 4718596
  402.8 55.1 %collective-permute-start.4 = (bf16[4,2,2,48,1536]{4,3,2,1,0:T(8,128)(2,1)S(1)}, bf16[4,2,2,48,1536]{4,3,2,1,0:T(8,128)(2,1)S(1)}, u32[]{:S(2)}, u32[]{:S(2)}) collective-permute-start(bf16[4,2,2,48,1536]{4,3,2,1,0:T(8,128)(2,1)S(1)} %fusion.17), channel_id=1, source_target_pairs={{0,2},{2,0},{4,6},{6,4},{8,10},{10,8},{12,14},{14,12},{16,18},{18,... | collective-permute-start | bytes 7077896 | tf_op jit(solution)/shard_map/ppermute | solution.py:170
  434.0 9.6 %collective-permute-start.12 = (bf16[4,48,1024]{2,1,0:T(8,128)(2,1)S(1)}, bf16[4,48,1024]{2,1,0:T(8,128)(2,1)S(1)}, u32[]{:S(2)}, u32[]{:S(2)}) collective-permute-start(bf16[4,48,1024]{2,1,0:T(8,128)(2,1)S(1)} %dynamic-slice_bitcast_fusion.10), channel_id=1, source_target_pairs={{0,4},{2,6},{4,0},{6,2},{8,12},{10,14},{12,8},{14,10},{16,20},{18,... | collective-permute-start | bytes 1179656 | tf_op jit(solution)/shard_map/ppermute | solution.py:170
  435.4 4.9 copy-start.13
  440.4 48.7 %collective-permute-start.22 = (bf16[4,2,2,128,1024]{4,3,2,1,0:T(8,128)(2,1)}, bf16[4,2,2,128,1024]{4,3,2,1,0:T(8,128)(2,1)}, u32[]{:S(2)}, u32[]{:S(2)}) collective-permute-start(bf16[4,2,2,128,1024]{4,3,2,1,0:T(8,128)(2,1)} %dynamic-slice_bitcast_fusion), channel_id=1, source_target_pairs={{0,2},{2,0},{4,6},{6,4},{8,10},{10,8},{12,14},{14,12},{16,18},{18,... | collective-permute-start | bytes 12582920 | tf_op jit(solution)/shard_map/ppermute | solution.py:170
  441.7 12.0 %copy-start.4 = (f32[512,1024]{1,0:T(8,128)S(1)}, f32[512,1024]{1,0:T(8,128)}, u32[]{:S(2)}) copy-start(f32[512,1024]{1,0:T(8,128)} %copy-done.3) | copy-start | bytes 6291460
  443.7 4.7 collective-permute-start.15
  446.1 9.2 %collective-permute-start.14 = (bf16[48,1024]{1,0:T(8,128)(2,1)S(1)}, bf16[48,1024]{1,0:T(8,128)(2,1)S(1)}, u32[]{:S(2)}, u32[]{:S(2)}) collective-permute-start(bf16[48,1024]{1,0:T(8,128)(2,1)S(1)} %get-tuple-element.99), channel_id=1, source_target_pairs={{0,16},{2,18},{4,20},{6,22},{8,24},{10,26},{12,28},{14,30},{16,0},... | collective-permute-start | bytes 294920 | tf_op jit(solution)/shard_map/ppermute | solution.py:196
  448.4 7.5 %collective-permute-start.13 = (bf16[48,1024]{1,0:T(8,128)(2,1)S(1)}, bf16[48,1024]{1,0:T(8,128)(2,1)S(1)}, u32[]{:S(2)}, u32[]{:S(2)}) collective-permute-start(bf16[48,1024]{1,0:T(8,128)(2,1)S(1)} %get-tuple-element.97), channel_id=1, source_target_pairs={{0,8},{2,10},{4,12},{6,14},{8,16},{10,18},{12,20},{14,22},{16,24},... | collective-permute-start | bytes 294920 | tf_op jit(solution)/shard_map/ppermute | solution.py:196
  458.0 31.1 %slice-start = ((s8[8388608]{0:T(1024)(128)(4,1)}), s8[4194304]{0:T(1024)(128)(4,1)S(1)}, s32[]{:S(2)}) async-start(s8[8388608]{0:T(1024)(128)(4,1)} %bitcast.233), calls=%async_computation.3 | async-start | bytes 8388608
  458.8 30.3 %slice-start.1 = ((s8[8388608]{0:T(1024)(128)(4,1)}), s8[4194304]{0:T(1024)(128)(4,1)S(1)}, s32[]{:S(2)}) async-start(s8[8388608]{0:T(1024)(128)(4,1)} %bitcast.233), calls=%async_computation.4 | async-start | bytes 8388608
  458.8 24.7 %collective-permute-start.5 = (bf16[4,2,48,1536]{3,2,1,0:T(8,128)(2,1)S(1)}, bf16[4,2,48,1536]{3,2,1,0:T(8,128)(2,1)S(1)}, u32[]{:S(2)}, u32[]{:S(2)}) collective-permute-start(bf16[4,2,48,1536]{3,2,1,0:T(8,128)(2,1)S(1)} %dynamic-slice_bitcast_fusion.5), channel_id=1, source_target_pairs={{0,4},{2,6},{4,0},{6,2},{8,12},{10,14},{12,8},{14,10},{16,20},{18,... | collective-permute-start | bytes 3538952 | tf_op jit(solution)/shard_map/ppermute | solution.py:170
  465.6 46.3 %collective-permute-start.17 = (bf16[4,2,32,4096]{3,2,1,0:T(8,128)(2,1)S(1)}, bf16[4,2,32,4096]{3,2,1,0:T(8,128)(2,1)S(1)}, u32[]{:S(2)}, u32[]{:S(2)}) collective-permute-start(bf16[4,2,32,4096]{3,2,1,0:T(8,128)(2,1)S(1)} %dynamic-slice_bitcast_fusion.3), channel_id=1, source_target_pairs={{0,1},{1,0},{2,3},{3,2},{4,5},{5,4},{6,7},{7,6},{8,9},{9,8},{10,11... | collective-permute-start | bytes 6291464 | tf_op jit(solution)/shard_map/ppermute | solution.py:170
  484.8 9.8 %collective-permute-start.8 = (bf16[2,48,1536]{2,1,0:T(8,128)(2,1)}, bf16[2,48,1536]{2,1,0:T(8,128)(2,1)}, u32[]{:S(2)}, u32[]{:S(2)}) collective-permute-start(bf16[2,48,1536]{2,1,0:T(8,128)(2,1)} %get-tuple-element.79), channel_id=1, source_target_pairs={{0,24},{2,26},{4,28},{6,30},{8,0},{10,2},{12,4},{14,6},{16,8},{18,... | collective-permute-start | bytes 884744 | tf_op jit(solution)/shard_map/ppermute | solution.py:196
  486.8 23.1 %collective-permute-start.7 = (bf16[2,48,1536]{2,1,0:T(8,128)(2,1)}, bf16[2,48,1536]{2,1,0:T(8,128)(2,1)}, u32[]{:S(2)}, u32[]{:S(2)}) collective-permute-start(bf16[2,48,1536]{2,1,0:T(8,128)(2,1)} %get-tuple-element.80), channel_id=1, source_target_pairs={{0,16},{2,18},{4,20},{6,22},{8,24},{10,26},{12,28},{14,30},{16,0},... | collective-permute-start | bytes 884744 | tf_op jit(solution)/shard_map/ppermute | solution.py:196
  487.1 22.8 %collective-permute-start.6 = (bf16[2,48,1536]{2,1,0:T(8,128)(2,1)S(1)}, bf16[2,48,1536]{2,1,0:T(8,128)(2,1)}, u32[]{:S(2)}, u32[]{:S(2)}) collective-permute-start(bf16[2,48,1536]{2,1,0:T(8,128)(2,1)S(1)} %get-tuple-element.78), channel_id=1, source_target_pairs={{0,8},{2,10},{4,12},{6,14},{8,16},{10,18},{12,20},{14,22},{16,24},... | collective-permute-start | bytes 884744 | tf_op jit(solution)/shard_map/ppermute | solution.py:196
  493.6 48.6 %collective-permute-start.23 = (bf16[4,2,128,1024]{3,2,1,0:T(8,128)(2,1)S(1)}, bf16[4,2,128,1024]{3,2,1,0:T(8,128)(2,1)S(1)}, u32[]{:S(2)}, u32[]{:S(2)}) collective-permute-start(bf16[4,2,128,1024]{3,2,1,0:T(8,128)(2,1)S(1)} %dynamic-slice_bitcast_fusion.2), channel_id=1, source_target_pairs={{0,4},{2,6},{4,0},{6,2},{8,12},{10,14},{12,8},{14,10},{16,20},{18,... | collective-permute-start | bytes 6291464 | tf_op jit(solution)/shard_map/ppermute | solution.py:170
  511.2 5.2 collective-permute-start.9
  512.9 46.2 %collective-permute-start.18 = (bf16[4,32,4096]{2,1,0:T(8,128)(2,1)S(1)}, bf16[4,32,4096]{2,1,0:T(8,128)(2,1)S(1)}, u32[]{:S(2)}, u32[]{:S(2)}) collective-permute-start(bf16[4,32,4096]{2,1,0:T(8,128)(2,1)S(1)} %dynamic-slice_bitcast_fusion.7), channel_id=1, source_target_pairs={{0,4},{2,6},{4,0},{6,2},{8,12},{10,14},{12,8},{14,10},{16,20},{18,... | collective-permute-start | bytes 3145736 | tf_op jit(solution)/shard_map/ppermute | solution.py:170
  543.3 19.5 %collective-permute-start.24 = (bf16[4,128,1024]{2,1,0:T(8,128)(2,1)S(1)}, bf16[4,128,1024]{2,1,0:T(8,128)(2,1)S(1)}, u32[]{:S(2)}, u32[]{:S(2)}) collective-permute-start(bf16[4,128,1024]{2,1,0:T(8,128)(2,1)S(1)} %dynamic-slice_bitcast_fusion.6), channel_id=1, source_target_pairs={{0,1},{1,0},{2,3},{3,2},{4,5},{5,4},{6,7},{7,6},{8,9},{9,8},{10,11... | collective-permute-start | bytes 3145736 | tf_op jit(solution)/shard_map/ppermute | solution.py:170
  559.5 11.6 %collective-permute-start.21 = (bf16[32,4096]{1,0:T(8,128)(2,1)S(1)}, bf16[32,4096]{1,0:T(8,128)(2,1)S(1)}, u32[]{:S(2)}, u32[]{:S(2)}) collective-permute-start(bf16[32,4096]{1,0:T(8,128)(2,1)S(1)} %get-tuple-element.85), channel_id=1, source_target_pairs={{0,24},{2,26},{4,28},{6,30},{8,0},{10,2},{12,4},{14,6},{16,8},{18,... | collective-permute-start | bytes 786440 | tf_op jit(solution)/shard_map/ppermute | solution.py:196
  561.7 33.1 %collective-permute-start.20 = (bf16[32,4096]{1,0:T(8,128)(2,1)S(1)}, bf16[32,4096]{1,0:T(8,128)(2,1)S(1)}, u32[]{:S(2)}, u32[]{:S(2)}) collective-permute-start(bf16[32,4096]{1,0:T(8,128)(2,1)S(1)} %get-tuple-element.86), channel_id=1, source_target_pairs={{0,16},{2,18},{4,20},{6,22},{8,24},{10,26},{12,28},{14,30},{16,0},... | collective-permute-start | bytes 786440 | tf_op jit(solution)/shard_map/ppermute | solution.py:196
  562.5 32.2 %collective-permute-start.19 = (bf16[32,4096]{1,0:T(8,128)(2,1)S(1)}, bf16[32,4096]{1,0:T(8,128)(2,1)S(1)}, u32[]{:S(2)}, u32[]{:S(2)}) collective-permute-start(bf16[32,4096]{1,0:T(8,128)(2,1)S(1)} %get-tuple-element.84), channel_id=1, source_target_pairs={{0,8},{2,10},{4,12},{6,14},{8,16},{10,18},{12,20},{14,22},{16,24},... | collective-permute-start | bytes 786440 | tf_op jit(solution)/shard_map/ppermute | solution.py:196
  563.3 32.4 %collective-permute-start.27 = (bf16[128,1024]{1,0:T(8,128)(2,1)S(1)}, bf16[128,1024]{1,0:T(8,128)(2,1)S(1)}, u32[]{:S(2)}, u32[]{:S(2)}) collective-permute-start(bf16[128,1024]{1,0:T(8,128)(2,1)S(1)} %get-tuple-element.82), channel_id=1, source_target_pairs={{0,24},{2,26},{4,28},{6,30},{8,0},{10,2},{12,4},{14,6},{16,8},{18,... | collective-permute-start | bytes 786440 | tf_op jit(solution)/shard_map/ppermute | solution.py:196
  566.9 36.1 %collective-permute-start.26 = (bf16[128,1024]{1,0:T(8,128)(2,1)S(1)}, bf16[128,1024]{1,0:T(8,128)(2,1)S(1)}, u32[]{:S(2)}, u32[]{:S(2)}) collective-permute-start(bf16[128,1024]{1,0:T(8,128)(2,1)S(1)} %get-tuple-element.83), channel_id=1, source_target_pairs={{0,16},{2,18},{4,20},{6,22},{8,24},{10,26},{12,28},{14,30},{16,0},... | collective-permute-start | bytes 786440 | tf_op jit(solution)/shard_map/ppermute | solution.py:196
  571.1 31.9 %collective-permute-start.25 = (bf16[128,1024]{1,0:T(8,128)(2,1)S(1)}, bf16[128,1024]{1,0:T(8,128)(2,1)S(1)}, u32[]{:S(2)}, u32[]{:S(2)}) collective-permute-start(bf16[128,1024]{1,0:T(8,128)(2,1)S(1)} %get-tuple-element.81), channel_id=1, source_target_pairs={{0,8},{2,10},{4,12},{6,14},{8,16},{10,18},{12,20},{14,22},{16,24},... | collective-permute-start | bytes 786440 | tf_op jit(solution)/shard_map/ppermute | solution.py:196
Sparse Core Ops, SparseCore 0:
  17.6 86.3 all-gather.8
  107.0 76.0 all-gather.4
  186.3 76.0 all-gather.6
